TPU v7x, 256 devices: a whole 4x4x8 slice. The times are simulated.
256 devices in a mesh: pool: 2 (over core), ep: 32 (over y, z), half: 4 (over x).
Axes of the slice: x: 4, y: 4, z: 8, core: 2. Of those that a mesh axis runs over, the one named last changes fastest.
Arguments:
- tokens: bfloat16 [2, 2048, 4096], P('pool', 'ep'), may hold values from -6 to 6
- routes: int32 [2, 2048, 8], P('pool', 'ep'), may hold values from 0 to 31, all different within a row; in each aligned block of 64 rows (0 to 63, 64 to 127, ..., all dimensions but the last counted through in order) at most 32 rows name the same one
- router: bfloat16 [4096, 32], replicated, may hold values from -0.03125 to 0.03125
- w_gate: bfloat16 [32, 4096, 1536], P('ep', None, 'half'), may hold values from -0.09375 to 0.09375
- w_up: bfloat16 [32, 4096, 1536], P('ep', None, 'half'), may hold values from -0.09375 to 0.09375
- w_down: bfloat16 [32, 1536, 4096], P('ep', 'half'), may hold values from -0.625 to 0.625
- norm_gain: float32 [4096], replicated, may hold values from 0.1 to 1.9
- w_kv: bfloat16 [4096, 2048], P('ep', 'half'), may hold values from -0.09375 to 0.09375
- lengths: int32 [2, 32, 2], P(None, 'ep'), may hold values from 1 to 48, 64 in all within a row
- queries: bfloat16 [2, 8192, 2048], P('pool', 'ep', 'half'), may hold values from -150 to 150
- new_keys: bfloat16 [2, 8192, 1024], P('pool', 'ep', 'half'), may hold values from -5 to 5
- new_values: bfloat16 [2, 8192, 1024], P('pool', 'ep', 'half'), may hold values from -6 to 6
- w_out: bfloat16 [2048, 2048], P('half'), may hold values from -0.125 to 0.125
Outputs:
- decoded: bfloat16 [2, 8192, 2048], P('pool', ('ep', 'half'))
Inputs may be any that keep to these rules, and one draw needn't show every extreme that they name: `routes`: each token names 8 different experts; within each aligned block of 64 tokens no expert is named by more than 32 tokens. The 2 lengths of a group sum to 64.
All inputs are finite; a program needn't handle non-finite values.
Results may differ from a plain program's by a relative error of at most 0.022.
Values may be sent and summed in bfloat16 or wider, within the bound.
A program may use at most 128 MiB of HBM per device.

v0:
```python
import math

import jax
import jax.numpy as jnp
from jax import lax
from jax.sharding import PartitionSpec as P

HEAD = 128
SAMPLES = 128
CAP = 32


def from_partner(shard, axis, stride):
    return lax.ppermute(shard, axis, [(i, i ^ 1 << stride) for i in range(lax.axis_size(axis))])


def expand(form, rows, w_gate, w_up):
    gate = jnp.einsum(form, rows, w_gate, preferred_element_type=jnp.float32)
    up = jnp.einsum(form, rows, w_up, preferred_element_type=jnp.float32)
    return (jax.nn.silu(gate) * up).astype(jnp.bfloat16)


def attend(block, prompt_lengths, query, fresh_key, fresh_value):
    group_tok = block.shape[0]
    group_rows = query.shape[0]
    ends = jnp.cumsum(prompt_lengths)
    position = jnp.arange(group_tok, dtype=jnp.int32)
    segment = jnp.sum((position[:, None] >= ends[None, :]).astype(jnp.int32), axis=1)
    prompt = jnp.arange(group_rows, dtype=jnp.int32) // SAMPLES
    allowed = segment[None, :] == prompt[:, None]
    keys = block[:, :, 0, :]
    values = block[:, :, 1, :]
    scale = 1.0 / math.sqrt(HEAD)
    scores = jnp.einsum("rhgd,thd->rhgt", query, keys, preferred_element_type=jnp.float32) * scale
    scores = jnp.where(allowed[:, None, None, :], scores, -1e30)
    own = jnp.einsum("rhgd,rhd->rhg", query, fresh_key, preferred_element_type=jnp.float32) * scale
    top = jnp.maximum(jnp.max(scores, axis=3), own)
    spread = jnp.where(allowed[:, None, None, :], jnp.exp(scores - top[..., None]), 0.0)
    self_weight = jnp.exp(own - top)
    total = jnp.sum(spread, axis=3) + self_weight
    probs = (spread / total[..., None]).astype(jnp.bfloat16)
    self_prob = (self_weight / total).astype(jnp.bfloat16)
    mixed = jnp.einsum("rhgt,thd->rhgd", probs, values, preferred_element_type=jnp.float32)
    mixed = (
        mixed
        + self_prob.astype(jnp.float32)[..., None] * fresh_value.astype(jnp.float32)[:, :, None, :]
    )
    return mixed.astype(jnp.bfloat16).reshape(group_rows, -1)


def on_device(
    tokens,
    routes,
    router,
    w_gate,
    w_up,
    w_down,
    norm_gain,
    w_kv,
    lengths,
    queries,
    new_keys,
    new_values,
    w_out,
):
    inputs = tokens[0]
    chosen = routes[0]
    experts = router.shape[1]
    local_experts = w_gate.shape[0]
    model = inputs.shape[1]
    ep_count = lax.axis_size("ep")
    half_count = lax.axis_size("half")
    feature_rows = model // half_count
    logits = jnp.dot(inputs, router, preferred_element_type=jnp.float32)
    picked = jnp.take_along_axis(logits, chosen, axis=1)
    weights = jax.nn.softmax(picked, axis=1).reshape(-1)
    flat = chosen.reshape(-1)
    onehot = (flat[:, None] == jnp.arange(experts, dtype=jnp.int32)[None, :]).astype(jnp.int32)
    before = jnp.cumsum(onehot, axis=0) - onehot
    rank = jnp.sum(before * onehot, axis=1)
    slot = flat * CAP + rank
    select = (slot[:, None] == jnp.arange(experts * CAP, dtype=jnp.int32)[None, :]).astype(
        jnp.bfloat16
    )
    select = jnp.sum(select.reshape(inputs.shape[0], -1, experts * CAP), axis=1)
    outgoing = jnp.einsum("ts,td->sd", select, inputs, preferred_element_type=jnp.float32).astype(
        jnp.bfloat16
    )
    outgoing = outgoing.reshape(ep_count, local_experts, CAP, model)
    received = lax.all_to_all(outgoing, "ep", split_axis=0, concat_axis=0, tiled=True)
    hidden = expand("secd,edf->escf", received, w_gate, w_up)
    hidden = hidden.reshape(local_experts, ep_count * CAP, -1)
    columns = w_down
    summed = lax.psum_scatter(
        jnp.einsum("erf,efd->der", hidden, columns, preferred_element_type=jnp.float32).astype(
            jnp.bfloat16
        ),
        "half",
        scatter_dimension=0,
        tiled=True,
    ).astype(jnp.float32)
    summed = summed.astype(jnp.bfloat16).reshape(feature_rows, local_experts, ep_count, CAP)
    back = lax.all_to_all(summed, "ep", split_axis=2, concat_axis=2, tiled=True)
    flat_back = back.reshape(feature_rows, -1)
    column = flat % local_experts * (ep_count * CAP) + flat // local_experts * CAP + rank
    arrived = flat_back[:, column].astype(jnp.float32)
    weighted = jnp.sum(
        (arrived * weights[None, :]).reshape(feature_rows, inputs.shape[0], -1), axis=2
    )
    moe_whole = lax.all_gather(weighted.T.astype(jnp.bfloat16), "half", axis=1, tiled=True).astype(
        jnp.float32
    )
    mixed = inputs.astype(jnp.float32) + moe_whole
    meansq = jnp.mean(mixed * mixed, axis=1, keepdims=True)
    normed = (mixed * lax.rsqrt(meansq + 1e-06) * norm_gain).astype(jnp.bfloat16)
    columns = normed
    keyvals = jnp.dot(
        columns, lax.all_gather(w_kv, "ep", axis=0, tiled=True), preferred_element_type=jnp.float32
    ).astype(jnp.bfloat16)
    remote = from_partner(keyvals, "pool", 0)
    other = 1 - lax.axis_index("pool")
    prompt_lengths = lax.dynamic_index_in_dim(lengths, other, 0, keepdims=False)[0]
    kv_heads = new_keys.shape[2] // HEAD
    block = remote.reshape(remote.shape[0], kv_heads, 2, HEAD)
    query = queries[0].reshape(queries.shape[1], kv_heads, -1, HEAD)
    fresh_key = new_keys[0].reshape(new_keys.shape[1], kv_heads, HEAD)
    fresh_value = new_values[0].reshape(new_values.shape[1], kv_heads, HEAD)
    attention = attend(block, prompt_lengths, query, fresh_key, fresh_value)
    decoded = lax.psum_scatter(
        jnp.dot(attention, w_out, preferred_element_type=jnp.float32).astype(jnp.bfloat16),
        "half",
        scatter_dimension=0,
        tiled=True,
    )
    return decoded[None]


def solution(mesh):
    in_specs = (
        P("pool", "ep", None),
        P("pool", "ep", None),
        P(),
        P("ep", None, "half"),
        P("ep", None, "half"),
        P("ep", "half", None),
        P(),
        P("ep", "half"),
        P(None, "ep", None),
        P("pool", "ep", "half"),
        P("pool", "ep", "half"),
        P("pool", "ep", "half"),
        P("half", None),
    )
    out_specs = P("pool", ("ep", "half"), None)
    return jax.shard_map(
        on_device, mesh=mesh, in_specs=in_specs, out_specs=out_specs, check_vma=False
    )
```

profile of v0, /device:TPU:8, one launch (start us, length us, event | category | flops | bytes accessed | tf_op | source)
XLA Modules:
  0.0 430.7 jit_solution(18236778553920500972)
XLA Ops:
  7.4 0.9 copy.42
  8.5 1.2 reduce-window.18
  9.7 0.2 slice_reduce_fusion
  10.1 0.7 fusion.17
  10.8 3.4 convolution_convert_fusion
  14.3 195.1 %all_to_all.10 = bf16[32,1,32,4096]{3,2,1,0:T(8,128)(2,1)S(1)} all-to-all(bf16[32,1,32,4096]{3,2,1,0:T(8,128)(2,1)S(1)} %bitcast.143), channel_id=1, replica_groups=mesh['pool'=2,'ep'=32,'half'=4] {'ep'}, dimensions={0} | all-to-all | bytes 16777216 | tf_op jit(solution)/shard_map/all_to_all | solution.py:90
  209.4 4.5 %fusion.2 = f32[32,32,384]{2,1,0:T(8,128)S(1)} fusion(bf16[32,1,32,4096]{3,2,1,0:T(8,128)(2,1)S(1)} %all_to_all.10, bf16[1,4096,384]{2,1,0:T(8,128)(2,1)S(1)} %copy-done.6), kind=kOutput, calls=%fused_computation.4 | convolution fusion | flops 3221225472 | bytes 13107200 | tf_op jit(solution)/shard_map/secd,edf->escf/dot_general | solution.py:18
  213.9 4.6 %multiply_convert_fusion = bf16[32,32,384]{2,1,0:T(8,128)(2,1)S(1)} fusion(f32[32,32,384]{2,1,0:T(8,128)S(1)} %fusion.2, bf16[1,4096,384]{2,1,0:T(8,128)(2,1)S(1)} %copy-done.7, bf16[32,1,32,4096]{3,2,1,0:T(8,128)(2,1)S(1)} %all_to_all.10), kind=kOutput, calls=%fused_computation.16 | convolution fusion | flops 3223584768 | bytes 13893632 | tf_op jit(solution)/shard_map/secd,edf->escf/dot_general | solution.py:19
  218.5 6.7 %convert_bitcast_fusion = bf16[4096,1,1024]{0,2,1:T(8,128)(2,1)} fusion(bf16[1024,384]{1,0:T(8,128)(2,1)S(1)} %bitcast.150, bf16[1,384,4096]{2,1,0:T(8,128)(2,1)S(1)} %copy-done), kind=kOutput, calls=%fused_computation.6 | convolution fusion | flops 3225419776 | bytes 12320768 | tf_op jit(solution)/shard_map/erf,efd->der/dot_general | solution.py:95
  225.3 0.5 all-gather.2.cloned.1.call-update
  225.8 81.4 %reduce-scatter.3.cloned.1.call-done = bf16[1024,1,1024]{0,2,1:T(8,128)(2,1)} async-done(((bf16[4096,1,1024]{0,2,1:T(8,128)(2,1)}), bf16[1024,1,1024]{0,2,1:T(8,128)(2,1)}) %reduce-scatter.3.cloned.1.call-update) | async-done | bytes 2097168 | tf_op jit(solution)/shard_map/reduce_scatter | solution.py:94
  307.2 10.2 %all-to-all-start.1 = ((bf16[1024,1,32,32]{0,3,1,2:T(8,128)(2,1)}), bf16[1024,1,32,32]{0,3,1,2:T(8,128)(2,1)}, u32[]{:S(2)}, u32[]{:S(2)}) async-start(bf16[1024,1,32,32]{0,3,1,2:T(8,128)(2,1)} %bitcast.144), calls=%async_computation.2 | async-start | bytes 4194304 | tf_op jit(solution)/shard_map/all_to_all | solution.py:103
  317.9 1.3 fusion.19
  319.2 3.9 gather_fusion.1
  323.4 1.0 reshape_squeeze.11
  324.4 1.9 reshape.307
  326.5 0.2 fusion.36
  326.8 2.4 fusion.48
  329.2 35.8 %all-to-all-done.1 = bf16[1024,1,32,32]{0,3,1,2:T(8,128)(2,1)} async-done(((bf16[1024,1,32,32]{0,3,1,2:T(8,128)(2,1)}), bf16[1024,1,32,32]{0,3,1,2:T(8,128)(2,1)}, u32[]{:S(2)}, u32[]{:S(2)}) %all-to-all-start.1) | async-done | bytes 2097184 | tf_op jit(solution)/shard_map/all_to_all | solution.py:103
  365.0 5.4 %gather_fusion = bf16[512,1024]{1,0:T(8,128)(2,1)} fusion(bf16[1024,1024]{0,1:T(8,128)(2,1)} %bitcast.16, s32[1024]{0:T(1024)S(1)} %pad_clamp_fusion), kind=kCustom, calls=%fused_computation | custom fusion | bytes 2099200 | tf_op jit(solution)/shard_map/gather | solution.py:106
  370.4 1.9 fusion.7
  372.3 12.8 %all_gather.6 = bf16[64,4096]{1,0:T(8,128)(2,1)S(1)} all-gather(bf16[64,1024]{1,0:T(8,128)(2,1)S(1)} %bitcast.145), channel_id=1, replica_groups=mesh['pool'=2,'ep'=32,'half'=4] {'half'}, dimensions={1}, use_global_device_ids=true | all-gather | bytes 655360 | tf_op jit(solution)/shard_map/all_gather | solution.py:110
  385.1 0.8 copy-done.1
  385.9 1.3 multiply_reduce_fusion
  387.3 3.4 convolution_convert_fusion.2
  390.9 1.1 copy.56
  391.9 1.7 copy.58
  393.7 0.9 reshape.280
  394.6 0.2 fusion.47
  395.0 1.4 fusion.14
  396.4 1.7 convolution_convert_fusion.1
  398.1 25.2 %reduce-scatter.5.cloned.1.call-done = bf16[64,2048]{1,0:T(8,128)(2,1)} async-done(((bf16[256,2048]{1,0:T(8,128)(2,1)}), bf16[64,2048]{1,0:T(8,128)(2,1)}) %reduce-scatter.5.cloned.1.call-update) | async-done | bytes 262160 | tf_op jit(solution)/shard_map/reduce_scatter | solution.py:129
  (54 shorter events, 1.9 us)
Async XLA Ops:
  7.4 211.1 %copy-start = (bf16[1,384,4096]{2,1,0:T(8,128)(2,1)S(1)}, bf16[1,384,4096]{2,1,0:T(8,128)(2,1)}, u32[]{:S(2)}) copy-start(bf16[1,384,4096]{2,1,0:T(8,128)(2,1)} %param.18) | copy-start | bytes 9437188
  7.4 299.8 %reduce-scatter.3.cloned.1.call-start = ((), (), s32[]{:S(2)}) async-start(), calls=%async_computation.4 | async-start | bytes 10485760 | tf_op jit(solution)/shard_map/reduce_scatter | solution.py:94
  14.3 195.2 %copy-start.6 = (bf16[1,4096,384]{2,1,0:T(8,128)(2,1)S(1)}, bf16[1,4096,384]{2,1,0:T(8,128)(2,1)}, u32[]{:S(2)}) copy-start(bf16[1,4096,384]{2,1,0:T(8,128)(2,1)} %param.16) | copy-start | bytes 9437188
  209.4 4.5 %copy-start.7 = (bf16[1,4096,384]{2,1,0:T(8,128)(2,1)S(1)}, bf16[1,4096,384]{2,1,0:T(8,128)(2,1)}, u32[]{:S(2)}) copy-start(bf16[1,4096,384]{2,1,0:T(8,128)(2,1)} %param.17) | copy-start | bytes 9437188
  225.2 92.3 %copy-start.4 = (s32[1,64,8]{1,2,0:T(8,128)S(1)}, s32[1,64,8]{1,2,0:T(8,128)}, u32[]{:S(2)}) copy-start(s32[1,64,8]{1,2,0:T(8,128)} %param.14) | copy-start | bytes 6148
  225.2 92.6 %copy-start.3 = (bf16[4096,32]{0,1:T(8,128)(2,1)S(1)}, bf16[4096,32]{0,1:T(8,128)(2,1)}, u32[]{:S(2)}) copy-start(bf16[4096,32]{0,1:T(8,128)(2,1)} %param.15) | copy-start | bytes 786436
  225.2 162.0 %all-gather.2.cloned.1.call-start = ((), (), s32[]{:S(2)}) async-start(), calls=%async_computation.5 | async-start | bytes 4325376 | tf_op jit(solution)/shard_map/all_gather | solution.py:118
  307.2 57.8 %all-to-all-start.1 = ((bf16[1024,1,32,32]{0,3,1,2:T(8,128)(2,1)}), bf16[1024,1,32,32]{0,3,1,2:T(8,128)(2,1)}, u32[]{:S(2)}, u32[]{:S(2)}) async-start(bf16[1024,1,32,32]{0,3,1,2:T(8,128)(2,1)} %bitcast.144), calls=%async_computation.2 | async-start | bytes 4194304 | tf_op jit(solution)/shard_map/all_to_all | solution.py:103
  317.4 105.9 %reduce-scatter.5.cloned.1.call-start = ((), (), s32[]{:S(2)}) async-start(), calls=%async_computation.6 | async-start | bytes 1310720 | tf_op jit(solution)/shard_map/reduce_scatter | solution.py:129
  319.2 4.0 copy-start.8
  365.0 22.3 %copy-start.5 = (f32[4096]{0:T(1024)S(1)}, f32[4096]{0:T(1024)}, u32[]{:S(2)}) copy-start(f32[4096]{0:T(1024)} %param.19) | copy-start | bytes 49156
  385.1 0.8 copy-start.1
  390.7 3.0 collective-permute-start
  394.5 1.9 copy-start.2
Sparse Core Ops, SparseCore 0:
  225.3 81.8 reduce-scatter.2
  398.3 25.0 reduce-scatter.4
Sparse Core Ops, SparseCore 1:
  228.3 79.7 all-gather.1
where the time goes:
time: 431 us
  blocking collectives  208 us (48%)
  waiting for transfers between devices  143 us (33%)
  matrix products  29.6 us (7%)
  local copies, waits for them, and re-layouts  18.6 us (4%)
  between operations  15.2 us (4%)
  starting transfers between devices  10.4 us (2%)
  other arithmetic  6.12 us (1%)
    all_to_all x1, blocking collectives, on_device(): lax.all_to_all(outgoing, 'ep', split_axis=0, concat_axis=0, tiled=True)  195 us
    reduce_scatter x1, waiting for transfers between devices, on_device(): lax.psum_scatter(jnp.einsum('erf,efd->der', hidden, columns, preferred_el...  81.4 us
    all_to_all x1, waiting for transfers between devices, on_device(): back = lax.all_to_all(summed, 'ep', split_axis=2, concat_axis=2, tiled=True)  35.8 us
    reduce_scatter x1, waiting for transfers between devices, on_device(): lax.psum_scatter(jnp.dot(attention, w_out, preferred_element_type=jnp.flo...  25.2 us
    all_gather x1, blocking collectives, on_device(): lax.all_gather(weighted.T.astype(jnp.bfloat16), 'half', axis=1, tiled=True)  12.8 us
    all_to_all x1, starting transfers between devices, on_device(): back = lax.all_to_all(summed, 'ep', split_axis=2, concat_axis=2, tiled=True)  10.2 us
  transfers between devices with their start and end apart: 5, of which 3 were waited for; matrix products, arithmetic and copies ran while one was open for 5% of the time, Pallas kernels for 0%

commit v1 on v0

v1 whole, which is shorter than its diff:
```python
import math

import jax
import jax.numpy as jnp
from jax import lax
from jax.experimental import pallas as pl
from jax.experimental.pallas import tpu as pltpu
from jax.sharding import PartitionSpec as P

HEAD = 128
SAMPLES = 128
CAP = 32
SLOTS = 16
MESH = pl.DeviceIdType.MESH
BF16 = jnp.bfloat16
F32 = jnp.float32


def moe_kernel(
    out_rows,
    combine,
    w_gate,
    w_up,
    w_down,
    result,
    w_in,
    w_out,
    mine,
    from_left,
    from_right,
    from_far,
    acc,
    hidden,
    partial,
    inbox,
    done,
    returned,
    piece,
    gathered,
    w_sem,
    local_sem,
    send_sem,
    recv_sem,
    ring_send,
    ring_recv,
    sum_send,
    sum_recv,
    back_local,
    back_send,
    back_recv,
    mix_send,
    mix_recv,
):
    chunks, n_ep, slots, quarter = out_rows.shape
    width = quarter // 2
    ff = w_gate.shape[1]
    half_groups = n_ep // 2
    half_rows = half_groups * slots
    tokens = combine.shape[1]
    ep = lax.axis_index("ep")
    x = lax.axis_index("half")
    right = lax.rem(x + 1, 4)
    left = lax.rem(x + 3, 4)
    far = lax.rem(x + 2, 4)

    loads = [
        pltpu.make_async_copy(w_gate, w_in.at[:, pl.ds(0, ff)], w_sem.at[0]),
        pltpu.make_async_copy(w_up, w_in.at[:, pl.ds(ff, ff)], w_sem.at[1]),
        pltpu.make_async_copy(w_down, w_out, w_sem.at[2]),
    ]
    for load in loads:
        load.start()

    barrier = pltpu.get_barrier_semaphore()

    @pl.loop(1, n_ep)
    def _(i):
        peer = lax.rem(ep + i, n_ep)
        pl.semaphore_signal(barrier, inc=1, device_id={"ep": peer}, device_id_type=MESH)

    for peer in (left, right, far):
        pl.semaphore_signal(barrier, inc=1, device_id={"half": peer}, device_id_type=MESH)
    pl.semaphore_wait(barrier, n_ep + 2)

    def stage(k):
        return k // 2, pl.ds(k % 2 * width, width)

    def half_of(ref, k, h):
        c, cols = stage(k)
        return ref.at[c, pl.ds(h * half_groups, half_groups), :, cols]

    def remote(src, dst, sems, recvs, where):
        return pltpu.make_async_remote_copy(
            src_ref=src,
            dst_ref=dst,
            send_sem=sems,
            recv_sem=recvs,
            device_id=where,
            device_id_type=MESH,
        )

    locals_ = []
    for k in range(4):
        c, cols = stage(k)

        @pl.loop(1, n_ep)
        def _(i, k=k, c=c, cols=cols):
            peer = lax.rem(ep + i, n_ep)
            remote(
                out_rows.at[c, peer, :, cols],
                mine.at[c, ep, :, cols],
                send_sem.at[k],
                recv_sem.at[k],
                {"ep": peer},
            ).start()

        own = pltpu.make_async_copy(
            out_rows.at[c, ep, :, cols], mine.at[c, ep, :, cols], local_sem.at[k]
        )
        own.start()
        locals_.append(own)

    def all_but_one(ref, k, sem):
        c, cols = stage(k)
        block = ref.at[c, pl.ds(0, n_ep - 1), :, cols]
        return pltpu.make_async_copy(block, block, sem.at[k])

    ring = {}

    def arrive(k):
        locals_[k].wait()
        all_but_one(mine, k, recv_sem).wait()
        plan = [
            (half_of(mine, k, 0), half_of(from_left, k, 0), right),
            (half_of(mine, k, 1), half_of(from_right, k, 1), left),
            (half_of(mine, k, 1), half_of(from_left, k, 1), right),
            (half_of(mine, k, 0), half_of(from_right, k, 0), left),
            (half_of(from_left, k, 0), half_of(from_far, k, 0), right),
            (half_of(from_right, k, 1), half_of(from_far, k, 1), left),
        ]
        ring[k] = [
            remote(src, dst, ring_send.at[k, j], ring_recv.at[k, j], {"half": where})
            for j, (src, dst, where) in enumerate(plan)
        ]
        for j in range(4):
            ring[k][j].start()

    def forward(k):
        ring[k][0].wait_recv()
        ring[k][4].start()
        ring[k][1].wait_recv()
        ring[k][5].start()

    def add(ref, k, h, owner, first=False):
        c, cols = stage(k)
        rows = ref[c, h * half_groups : (h + 1) * half_groups, :, k % 2 * width : (k % 2 + 1) * width]
        at = pl.multiple_of(owner * quarter + k % 2 * width, width)
        term = jnp.dot(
            rows.reshape(half_rows, width), w_in[pl.ds(at, width), :], preferred_element_type=F32
        )
        if first:
            acc[c, h] = term
        else:
            acc[c, h] += term

    def own(k):
        for h in range(2):
            add(mine, k, h, x, first=k % 2 == 0)

    def sides(k):
        add(from_left, k, 0, left)
        add(from_right, k, 1, right)
        ring[k][2].wait_recv()
        add(from_left, k, 1, left)
        ring[k][3].wait_recv()
        add(from_right, k, 0, right)

    def opposite(k):
        ring[k][4].wait_recv()
        add(from_far, k, 0, far)
        ring[k][5].wait_recv()
        add(from_far, k, 1, far)

    def activate(c):
        for h in range(2):
            gate = acc[c, h, :, :ff]
            up = acc[c, h, :, ff:]
            hidden[c, h] = (gate / (1.0 + jnp.exp(-gate)) * up).astype(BF16)

    def down(k, h, owner):
        at = pl.multiple_of(owner * quarter + k % 2 * width, width)
        return jnp.dot(hidden[k // 2, h], w_out[:, pl.ds(at, width)], preferred_element_type=F32)

    sums = {}

    def sum_start(k):
        sums[k] = [
            remote(
                partial.at[k, j],
                inbox.at[k, j],
                sum_send.at[k, j],
                sum_recv.at[k, j],
                {"half": right if j % 2 == 0 else left},
            )
            for j in range(6)
        ]
        for j, (owner, h) in enumerate([(far, 0), (far, 1), (right, 1), (left, 0)]):
            partial[k, j] = down(k, h, owner).astype(BF16)
            sums[k][j].start()

    def sum_middle(k):
        for j, (owner, h) in enumerate([(right, 0), (left, 1)]):
            term = down(k, h, owner)
            sums[k][j].wait_recv()
            partial[k, 4 + j] = (term + inbox[k, j].astype(F32)).astype(BF16)
            sums[k][4 + j].start()

    backs = {}

    def sum_end(k):
        c, cols = stage(k)
        for h, direct, through in ((0, 3, 4), (1, 2, 5)):
            term = down(k, h, x)
            sums[k][direct].wait_recv()
            term = term + inbox[k, direct].astype(F32)
            sums[k][through].wait_recv()
            term = (term + inbox[k, through].astype(F32)).astype(BF16)
            done[
                c,
                h * half_groups : (h + 1) * half_groups,
                :,
                k % 2 * width : (k % 2 + 1) * width,
            ] = term.reshape(half_groups, slots, width)

        @pl.loop(1, n_ep)
        def _(i):
            peer = lax.rem(ep + i, n_ep)
            remote(
                done.at[c, peer, :, cols],
                returned.at[c, ep, :, cols],
                back_send.at[k],
                back_recv.at[k],
                {"ep": peer},
            ).start()

        backs[k] = pltpu.make_async_copy(
            done.at[c, ep, :, cols], returned.at[c, ep, :, cols], back_local.at[k]
        )
        backs[k].start()

    def weigh(k):
        backs[k].wait()
        all_but_one(returned, k, back_recv).wait()
        c = k // 2
        rows = returned[c, :, :, k % 2 * width : (k % 2 + 1) * width].reshape(n_ep * slots, width)
        at = c * n_ep * slots
        gates = combine[:, :, at : at + n_ep * slots].reshape(2 * tokens, n_ep * slots)
        both = jnp.dot(gates, rows, preferred_element_type=F32)
        return both[:tokens] + both[tokens:]

    mixes = []

    def exchange(f, total):
        piece[f] = total.astype(BF16)
        for j, where in enumerate((right, left, far)):
            copy = remote(
                piece.at[f],
                gathered.at[f, j],
                mix_send.at[f, j],
                mix_recv.at[f, j],
                {"half": where},
            )
            copy.start()
            mixes.append(copy)

    arrive(0)
    for load in loads[:2]:
        load.wait()
    own(0)
    forward(0)
    arrive(1)
    sides(0)
    own(1)
    forward(1)
    opposite(0)
    arrive(2)
    sides(1)
    own(2)
    arrive(3)
    opposite(1)
    activate(0)
    loads[2].wait()
    sum_start(0)
    forward(2)
    own(3)
    sum_start(1)
    sum_middle(0)
    forward(3)
    sides(2)
    opposite(2)
    sum_middle(1)
    sum_end(0)
    sides(3)
    opposite(3)
    activate(1)
    sum_start(2)
    sum_end(1)
    sum_start(3)
    sum_middle(2)
    sum_middle(3)
    first = [weigh(0), weigh(1)]
    sum_end(2)
    sum_end(3)
    exchange(0, first[0] + weigh(2))
    exchange(1, first[1] + weigh(3))
    for copy in mixes:
        copy.wait_recv()
    for f in range(2):
        cols = slice(f * width, (f + 1) * width)
        result[x, :, cols] = piece[f]
        for j, owner in enumerate((left, right, far)):
            result[owner, :, cols] = gathered[f, j]
    for k in range(4):
        all_but_one(mine, k, send_sem).wait()
        all_but_one(mine, k, back_send).wait()
        for j in range(6):
            ring[k][j].wait_send()
            sums[k][j].wait_send()
    for copy in mixes:
        copy.wait_send()


def experts(out_rows, combine, w_gate, w_up, w_down):
    chunks, n_ep, slots, quarter = out_rows.shape
    model, ff = w_gate.shape
    tokens = combine.shape[1]
    width = quarter // 2
    half_rows = n_ep // 2 * slots
    rows = pltpu.VMEM((chunks, n_ep, slots, quarter), BF16)
    dma = pltpu.SemaphoreType.DMA
    vmem = pl.BlockSpec(memory_space=pltpu.VMEM)
    hbm = pl.BlockSpec(memory_space=pl.ANY)
    return pl.pallas_call(
        moe_kernel,
        out_shape=jax.ShapeDtypeStruct((4, tokens, quarter), BF16),
        in_specs=[vmem, vmem, hbm, hbm, hbm],
        out_specs=vmem,
        scratch_shapes=[
            pltpu.VMEM((model, 2 * ff), BF16),
            pltpu.VMEM((ff, model), BF16),
            rows,
            rows,
            rows,
            rows,
            pltpu.VMEM((chunks, 2, half_rows, 2 * ff), F32),
            pltpu.VMEM((chunks, 2, half_rows, ff), BF16),
            pltpu.VMEM((4, 6, half_rows, width), BF16),
            pltpu.VMEM((4, 6, half_rows, width), BF16),
            rows,
            rows,
            pltpu.VMEM((2, tokens, width), BF16),
            pltpu.VMEM((2, 3, tokens, width), BF16),
            dma((3,)),
            dma((4,)),
            dma((4,)),
            dma((4,)),
            dma((4, 6)),
            dma((4, 6)),
            dma((4, 6)),
            dma((4, 6)),
            dma((4,)),
            dma((4,)),
            dma((4,)),
            dma((2, 3)),
            dma((2, 3)),
        ],
        compiler_params=pltpu.CompilerParams(
            collective_id=0, has_side_effects=True, vmem_limit_bytes=56 * 2**20
        ),
        cost_estimate=pl.CostEstimate(
            flops=6 * chunks * n_ep * slots * model * ff,
            bytes_accessed=6 * model * ff + 500 * 2**20,
            transcendentals=chunks * n_ep * slots * ff,
        ),
        name="experts",
    )(out_rows, combine, w_gate, w_up, w_down)


def attend(block, prompt_lengths, query, fresh_key, fresh_value):
    group_tok = block.shape[0]
    group_rows = query.shape[0]
    position = jnp.arange(group_tok, dtype=jnp.int32)
    segment = (position >= prompt_lengths[0]).astype(jnp.int32)
    prompt = jnp.arange(group_rows, dtype=jnp.int32) // SAMPLES
    allowed = segment[None, :] == prompt[:, None]
    keys = block[:, :, 0, :]
    values = block[:, :, 1, :]
    scale = 1.0 / math.sqrt(HEAD)
    scores = jnp.einsum("rhgd,thd->rhgt", query, keys, preferred_element_type=F32) * scale
    scores = jnp.where(allowed[:, None, None, :], scores, -1e30)
    own = jnp.einsum("rhgd,rhd->rhg", query, fresh_key, preferred_element_type=F32) * scale
    top = jnp.maximum(jnp.max(scores, axis=3), own)
    spread = jnp.where(allowed[:, None, None, :], jnp.exp(scores - top[..., None]), 0.0)
    self_weight = jnp.exp(own - top)
    total = jnp.sum(spread, axis=3) + self_weight
    probs = (spread / total[..., None]).astype(BF16)
    self_prob = (self_weight / total).astype(BF16)
    mixed = jnp.einsum("rhgt,thd->rhgd", probs, values, preferred_element_type=F32)
    mixed = mixed + self_prob.astype(F32)[..., None] * fresh_value.astype(F32)[:, :, None, :]
    return mixed.astype(BF16).reshape(group_rows, -1)


def route(inputs, chosen, router, n_ep):
    count, top = chosen.shape
    pairs = count * top
    logits = jnp.dot(inputs, router, preferred_element_type=F32)
    onehot = chosen[:, :, None] == jnp.arange(n_ep, dtype=jnp.int32)
    picked = jnp.sum(jnp.where(onehot, logits[:, None, :], 0.0), axis=2)
    weights = jax.nn.softmax(picked, axis=1)
    flags = onehot.reshape(pairs, n_ep).astype(BF16)
    earlier = jnp.tri(pairs, pairs, -1, dtype=BF16)
    before = jnp.dot(earlier, flags, preferred_element_type=F32)
    rank = jnp.sum(before * flags.astype(F32), axis=1).astype(jnp.int32).reshape(count, top)
    slot = rank // SLOTS * (n_ep * SLOTS) + chosen * SLOTS + rank % SLOTS
    select = slot[:, :, None] == jnp.arange(n_ep * CAP, dtype=jnp.int32)
    combine = jnp.sum(jnp.where(select, weights[:, :, None], 0.0), axis=1)
    coarse = combine.astype(BF16)
    fine = (combine - coarse.astype(F32)).astype(BF16)
    return jnp.any(select, axis=1).astype(BF16), jnp.stack([coarse, fine])


def on_device(
    tokens,
    routes,
    router,
    w_gate,
    w_up,
    w_down,
    norm_gain,
    w_kv,
    lengths,
    queries,
    new_keys,
    new_values,
    w_out,
):
    inputs = tokens[0]
    n_ep = lax.axis_size("ep")
    quarter = inputs.shape[1] // lax.axis_size("half")
    select, combine = route(inputs, routes[0], router, n_ep)
    part = lax.dynamic_slice_in_dim(inputs, lax.axis_index("half") * quarter, quarter, 1)
    outgoing = jnp.einsum("ts,td->sd", select, part, preferred_element_type=F32).astype(BF16)
    outgoing = outgoing.reshape(CAP // SLOTS, n_ep, SLOTS, quarter)
    moe = experts(outgoing, combine, w_gate[0], w_up[0], w_down[0])
    moe = moe.transpose(1, 0, 2).reshape(inputs.shape)
    mixed = inputs.astype(F32) + moe.astype(F32)
    meansq = jnp.mean(mixed * mixed, axis=1, keepdims=True)
    normed = (mixed * lax.rsqrt(meansq + 1e-06) * norm_gain).astype(BF16)
    keyvals = jnp.dot(
        normed, lax.all_gather(w_kv, "ep", axis=0, tiled=True), preferred_element_type=F32
    ).astype(BF16)
    remote = lax.ppermute(keyvals, "pool", [(0, 1), (1, 0)])
    other = 1 - lax.axis_index("pool")
    prompt_lengths = lax.dynamic_index_in_dim(lengths, other, 0, keepdims=False)[0]
    kv_heads = new_keys.shape[2] // HEAD
    block = remote.reshape(remote.shape[0], kv_heads, 2, HEAD)
    query = queries[0].reshape(queries.shape[1], kv_heads, -1, HEAD)
    fresh_key = new_keys[0].reshape(new_keys.shape[1], kv_heads, HEAD)
    fresh_value = new_values[0].reshape(new_values.shape[1], kv_heads, HEAD)
    attention = attend(block, prompt_lengths, query, fresh_key, fresh_value)
    decoded = lax.psum_scatter(
        jnp.dot(attention, w_out, preferred_element_type=F32).astype(BF16),
        "half",
        scatter_dimension=0,
        tiled=True,
    )
    return decoded[None]


def solution(mesh):
    in_specs = (
        P("pool", "ep", None),
        P("pool", "ep", None),
        P(),
        P("ep", None, "half"),
        P("ep", None, "half"),
        P("ep", "half", None),
        P(),
        P("ep", "half"),
        P(None, "ep", None),
        P("pool", "ep", "half"),
        P("pool", "ep", "half"),
        P("pool", "ep", "half"),
        P("half", None),
    )
    out_specs = P("pool", ("ep", "half"), None)
    return jax.shard_map(
        on_device, mesh=mesh, in_specs=in_specs, out_specs=out_specs, check_vma=False
    )
```

time: 431 us -> 253 us (0.59)
  blocking collectives: 208 us -> 0 us
  Pallas kernels: 0 us -> 190 us
  waiting for transfers between devices: 143 us -> 23.4 us
  matrix products: 29.6 us -> 13.2 us
  local copies, waits for them, and re-layouts: 18.6 us -> 4.85 us
  starting transfers between devices: 10.4 us -> 0.04 us
    all_to_all x1 -> x0, blocking collectives: 195 us -> none  [on_device(): lax.all_to_all(outgoing, 'ep', split_axis=0, concat_axis=0, tiled=True)]
    pallas_call x0 -> x1, Pallas kernels: none -> 190 us  [experts(): pl.pallas_call(moe_kernel, out_shape=jax.ShapeDtypeStruct((4, tokens, qua...]
    reduce_scatter x2 -> x1, waiting for transfers between devices: 107 us -> 22.5 us  [on_device(): lax.psum_scatter(jnp.dot(attention, w_out, preferred_element_type=F32).as...]
    all_to_all x1 -> x0, waiting for transfers between devices: 35.8 us -> none  [on_device(): back = lax.all_to_all(summed, 'ep', split_axis=2, concat_axis=2, tiled=True)]
    dot_general x10 -> x8, matrix products: 29.6 us -> 13.2 us  [the longest x1 3.9 us: on_device(): jnp.dot(normed, lax.all_gather(w_kv, 'ep', axis=0, tiled=True), preferred...]
    all_gather x1 -> x0, blocking collectives: 12.8 us -> none  [on_device(): lax.all_gather(weighted.T.astype(jnp.bfloat16), 'half', axis=1, tiled=True)]
    all_to_all x1 -> x0, starting transfers between devices: 10.2 us -> none  [on_device(): back = lax.all_to_all(summed, 'ep', split_axis=2, concat_axis=2, tiled=True)]
    gather x5 -> x0, local copies, waits for them, and re-layouts: 9.51 us -> none  [the longest x1 5.36 us: on_device(): arrived = flat_back[:, column].astype(jnp.float32)]
  transfers between devices with their start and end apart: 5 -> 3, of which waited for: 3 -> 2; matrix products, arithmetic and copies ran while one was open for 5% -> 8% of each run, Pallas kernels for 0% -> 75%
where the time goes in v1:
time: 253 us
  Pallas kernels  190 us (75%)
  waiting for transfers between devices  23.4 us (9%)
  between operations  13.6 us (5%)
  matrix products  13.2 us (5%)
  other arithmetic  7.41 us (3%)
  local copies, waits for them, and re-layouts  4.85 us (2%)
    pallas_call x1, Pallas kernels, experts(): pl.pallas_call(moe_kernel, out_shape=jax.ShapeDtypeStruct((4, tokens, qua...  190 us
    reduce_scatter x1, waiting for transfers between devices, on_device(): lax.psum_scatter(jnp.dot(attention, w_out, preferred_element_type=F32).as...  22.5 us
  transfers between devices with their start and end apart: 3, of which 2 were waited for; matrix products, arithmetic and copies ran while one was open for 8% of the time, Pallas kernels for 75%

profile of v1, /device:TPU:8, one launch (start us, length us, event | category | flops | bytes accessed | tf_op | source)
XLA Modules:
  0.0 252.8 jit_solution(4850360531874912152)
XLA Ops:
  6.5 0.7 all-gather.2.cloned.1.call-update
  7.3 0.8 copy.29
  8.1 1.4 fusion.7
  9.4 0.7 select_reduce_fusion.1
  10.2 0.1 copy.32
  10.3 0.1 eq.54
  10.4 0.4 fusion.5
  10.8 0.1 convert_element_type.110
  11.0 0.7 select_reduce_fusion
  11.7 0.7 pad_maximum_fusion.combine
  12.5 0.7 fusion
  13.2 3.0 %convolution_convert_fusion.1 = bf16[1024,1024]{1,0:T(8,128)(2,1)} fusion(pred[64,1024]{1,0:T(8,128)(4,1)S(1)} %fusion, bf16[1,64,4096]{2,1,0:T(8,128)(2,1)} %param.13, s32[]{:T(128)S(6)} %select_n.53), kind=kOutput, calls=%fused_computation.4 | convolution fusion | flops 135266304 | bytes 2293764 | tf_op jit(solution)/shard_map/ts,td->sd/dot_general | solution.py:452
  16.2 190.2 %experts.1 = bf16[4,64,1024]{2,1,0:T(8,128)(2,1)} custom-call(bf16[2,32,16,1024]{3,2,1,0:T(8,128)(2,1)} %bitcast.84, bf16[2,64,1024]{2,1,0:T(8,128)(2,1)} %pad_maximum_fusion.combine, bf16[4096,384]{1,0:T(8,128)(2,1)} %bitcast.88, bf16[4096,384]{1,0:T(8,128)(2,1)} %bitcast.89, bf16[384,4096]{1,0:T(8,128)(2,1)} %bitcast.90), custom_call_target="tpu_custom_call" | custom-call | flops 9663676416 | bytes 533725184 | tf_op jit(solution)/shard_map/experts/pallas_call | solution.py:343
  206.4 1.2 convert_bitcast_fusion
  207.7 1.0 reshape_squeeze.7
  208.7 0.8 reshape.188
  209.5 0.7 constant_dynamic-slice_fusion
  210.1 0.6 compare_convert_fusion
  210.8 0.6 and_select_fusion
  211.3 1.3 multiply_reduce_fusion
  212.6 0.6 add_rsqrt_fusion
  213.2 2.3 fusion.39
  215.5 3.9 %convolution_convert_fusion.2 = bf16[64,512]{1,0:T(8,128)(2,1)} fusion(bf16[4096,512]{1,0:T(8,128)(2,1)} %all-gather.2.cloned.1.call-done, f32[64,4096]{1,0:T(8,128)S(1)} %bitcast.83, bf16[1,64,4096]{2,1,0:T(8,128)(2,1)} %param.13, f32[4096]{0:T(1024)S(1)} %copy-done.3, f32[64]{0:T(128)} %add_rsqrt_fusion), kind=kOutput, calls=%fused_computation.11 | convolution fusion | flops 269778944 | bytes 5849344 | tf_op jit(solution)/shard_map/dot_general | solution.py:459
  219.5 0.1 broadcast_compare_fusion
  219.5 1.1 copy.40
  220.6 0.1 copy.43
  220.7 0.2 collective-permute-done
  220.9 0.1 fusion.37
  221.0 0.2 fusion.38
  221.4 0.3 fusion.2
  221.7 1.7 convolution_convert_fusion
  223.4 22.5 %reduce-scatter.2.cloned.1.call-done = bf16[64,2048]{1,0:T(8,128)(2,1)} async-done(((bf16[256,2048]{1,0:T(8,128)(2,1)}), bf16[64,2048]{1,0:T(8,128)(2,1)}) %reduce-scatter.2.cloned.1.call-update) | async-done | bytes 262160 | tf_op jit(solution)/shard_map/reduce_scatter | solution.py:471
  (29 shorter events, 0.4 us)
Async XLA Ops:
  6.5 215.1 %copy-start = (bf16[512,2048]{1,0:T(8,128)(2,1)S(1)}, bf16[512,2048]{1,0:T(8,128)(2,1)}, u32[]{:S(2)}) copy-start(bf16[512,2048]{1,0:T(8,128)(2,1)} %param.25) | copy-start | bytes 6291460
  6.5 209.0 %all-gather.2.cloned.1.call-start = ((), (), s32[]{:S(2)}) async-start(), calls=%async_computation.1 | async-start | bytes 4325376 | tf_op jit(solution)/shard_map/all_gather | solution.py:460
  7.3 238.7 %reduce-scatter.2.cloned.1.call-start = ((), (), s32[]{:S(2)}) async-start(), calls=%async_computation.2 | async-start | bytes 1310720 | tf_op jit(solution)/shard_map/reduce_scatter | solution.py:471
  206.4 2.3 copy-start.1
  208.7 6.8 %copy-start.3 = (f32[4096]{0:T(1024)S(1)}, f32[4096]{0:T(1024)}, u32[]{:S(2)}) copy-start(f32[4096]{0:T(1024)} %param.19) | copy-start | bytes 49156
  215.5 5.1 %copy-start.2 = (bf16[1,256,256]{2,1,0:T(8,128)(2,1)S(1)}, bf16[1,256,256]{2,1,0:T(8,128)(2,1)}, u32[]{:S(2)}) copy-start(bf16[1,256,256]{2,1,0:T(8,128)(2,1)} %param.24) | copy-start | bytes 393220
  215.5 3.9 %copy-start.4 = (s32[256]{0:T(256)S(1)}, s32[256]{0:T(256)}, u32[]{:S(2)}) copy-start(s32[256]{0:T(256)} %and_select_fusion) | copy-start | bytes 3076
  215.5 3.9 %copy-start.5 = (s32[64]{0:T(128)S(1)}, s32[64]{0:T(128)}, u32[]{:S(2)}) copy-start(s32[64]{0:T(128)} %compare_convert_fusion) | copy-start | bytes 772
  219.4 1.5 collective-permute-start
Sparse Core Ops, SparseCore 0:
  10.0 93.0 all-gather.1
  223.5 22.3 reduce-scatter.1

commit v2 on v1

v2 whole, which is shorter than its diff:
```python
import math

import jax
import jax.numpy as jnp
from jax import lax
from jax.experimental import pallas as pl
from jax.experimental.pallas import tpu as pltpu
from jax.sharding import PartitionSpec as P

HEAD = 128
SAMPLES = 128
CAP = 32
SLOTS = 16
RING = 8
MESH = pl.DeviceIdType.MESH
BF16 = jnp.bfloat16
F32 = jnp.float32


def moe_kernel(
    tok,
    select,
    gates,
    w_gate,
    w_up,
    w_down,
    result,
    w_in,
    w_out,
    held,
    chosen,
    weights,
    picked,
    mine,
    direct,
    from_left,
    from_right,
    from_far,
    acc,
    hidden,
    partial,
    inbox,
    done,
    returned,
    blend,
    landed,
    piece,
    gathered,
    w_sem,
    tok_sem,
    zring_send,
    zring_recv,
    ctl_local,
    ctl_send,
    ctl_recv,
    y_local,
    y_send,
    y_recv,
    ring_send,
    ring_recv,
    sum_send,
    sum_recv,
    back_local,
    back_send,
    back_recv,
    down_local,
    down_send,
    down_recv,
    mix_send,
    mix_recv,
):
    tokens, columns = tok.shape
    xw = from_left.shape[3]
    dw = columns - xw
    width = xw // 2
    ff = w_gate.shape[1]
    n_ep = mine.shape[1]
    n_z = held.shape[0]
    n_y = n_ep // n_z
    half_groups = n_ep // 2
    half_rows = half_groups * SLOTS
    stripes = partial.shape[1]
    stripe = xw // stripes
    lanes = 2 * n_y * SLOTS
    ep = lax.axis_index("ep")
    y = ep // n_z
    z = lax.rem(ep, n_z)
    x = lax.axis_index("half")
    right = lax.rem(x + 1, 4)
    left = lax.rem(x + 3, 4)
    far = lax.rem(x + 2, 4)

    def at_z(i):
        return {"ep": y * n_z + lax.rem(z + i, n_z)}

    def at_y(i):
        return {"ep": lax.rem(y + i, n_y) * n_z + z}

    loads = [
        pltpu.make_async_copy(w_gate, w_in.at[:, pl.ds(0, ff)], w_sem.at[0]),
        pltpu.make_async_copy(w_up, w_in.at[:, pl.ds(ff, ff)], w_sem.at[1]),
        pltpu.make_async_copy(w_down, w_out, w_sem.at[2]),
    ]
    for load in loads:
        load.start()
    keep = pltpu.make_async_copy(tok, held.at[z], tok_sem)
    keep.start()

    barrier = pltpu.get_barrier_semaphore()

    def greet(where):
        pl.semaphore_signal(barrier, inc=1, device_id=where, device_id_type=MESH)

    @pl.loop(1, n_z)
    def _(i):
        greet(at_z(i))

    @pl.loop(1, n_y)
    def _(i):
        greet(at_y(i))

    for peer in (left, right, far):
        greet({"half": peer})
    pl.semaphore_wait(barrier, n_z + n_y + 1)

    def remote(src, dst, sems, recvs, where):
        return pltpu.make_async_remote_copy(
            src_ref=src,
            dst_ref=dst,
            send_sem=sems,
            recv_sem=recvs,
            device_id=where,
            device_id_type=MESH,
        )

    def wait_for(block, sem):
        pltpu.make_async_copy(block, block, sem).wait()

    parts = [(0, width), (width, width), (xw, dw // 2), (xw + dw // 2, dw // 2)]
    plus = n_z // 2
    minus = n_z - 1 - plus

    def round_copy(p, way, step):
        start, size = parts[p]
        cols = pl.ds(start, size)
        back = n_z - step if way == 0 else step
        block = lax.rem(z + back, n_z)
        src = tok.at[:, cols] if step == 0 else held.at[block, :, cols]
        return remote(
            src,
            held.at[block, :, cols],
            zring_send.at[p, way, step],
            zring_recv.at[p, way, step],
            at_z(1 if way == 0 else n_z - 1),
        )

    trips = {}

    def round_step(p, step):
        for way, steps in ((0, plus), (1, minus)):
            if 0 < step <= steps:
                trips[p, way, step - 1].wait_recv()
            if step < steps:
                trips[p, way, step] = round_copy(p, way, step)
                trips[p, way, step].start()

    def push_control(n, src, dst):
        @pl.loop(1, n_z)
        def _(i):
            there = pl.multiple_of(lax.rem(z + i, n_z) * lanes, lanes)
            remote(
                src.at[:, :, pl.ds(there, lanes)], dst.at[z], ctl_send.at[n], ctl_recv.at[n], at_z(i)
            ).start()

        here = pl.multiple_of(z * lanes, lanes)
        own = pltpu.make_async_copy(src.at[:, :, pl.ds(here, lanes)], dst.at[z], ctl_local.at[n])
        own.start()
        return own

    def wait_control(n, own, dst):
        own.wait()
        wait_for(dst.at[pl.ds(0, n_z - 1)], ctl_recv.at[n])

    def pick(start, size):
        @pl.loop(0, n_z)
        def _(s):
            rows = lax.dot_general(
                chosen[s, 0],
                held[s, :, start : start + size],
                (((0,), (0,)), ((), ())),
                preferred_element_type=F32,
            ).astype(BF16)
            rows = rows.reshape(2 * n_y, SLOTS, size)
            for b in range(2 * n_y):
                picked[b // n_y, b % n_y, s, :, start : start + size] = rows[b]

    y_own = {}

    def push_y(n, c, start, size, dst, dst_start):
        cols = pl.ds(start, size)
        there = dst.at[c, pl.ds(y * n_z, n_z), :, pl.ds(dst_start, size)]

        @pl.loop(1, n_y)
        def _(i):
            peer = lax.rem(y + i, n_y)
            remote(
                picked.at[c, peer, :, :, cols], there, y_send.at[n], y_recv.at[n], at_y(i)
            ).start()

        y_own[n] = pltpu.make_async_copy(picked.at[c, y, :, :, cols], there, y_local.at[n])
        y_own[n].start()

    def others(ref, c, start, size):
        return ref.at[c, pl.ds(0, n_ep - n_z), :, pl.ds(start, size)]

    def stage(k):
        return k // 2, pl.ds(k % 2 * width, width)

    def half_of(ref, k, h):
        c, cols = stage(k)
        return ref.at[c, pl.ds(h * half_groups, half_groups), :, cols]

    ring = {}

    def arrive(k):
        y_own[k].wait()
        wait_for(others(mine, k // 2, k % 2 * width, width), y_recv.at[k])
        plan = [
            (half_of(mine, k, 0), half_of(from_left, k, 0), right),
            (half_of(mine, k, 1), half_of(from_right, k, 1), left),
            (half_of(mine, k, 1), half_of(from_left, k, 1), right),
            (half_of(mine, k, 0), half_of(from_right, k, 0), left),
            (half_of(from_left, k, 0), half_of(from_far, k, 0), right),
            (half_of(from_right, k, 1), half_of(from_far, k, 1), left),
        ]
        ring[k] = [
            remote(src, dst, ring_send.at[k, j], ring_recv.at[k, j], {"half": where})
            for j, (src, dst, where) in enumerate(plan)
        ]
        for j in range(4):
            ring[k][j].start()

    def forward(k):
        ring[k][0].wait_recv()
        ring[k][4].start()
        ring[k][1].wait_recv()
        ring[k][5].start()

    def accumulate(ref, c, h, start, size, at, first=False):
        rows = ref[c, h * half_groups : (h + 1) * half_groups, :, start : start + size]
        term = jnp.dot(
            rows.reshape(half_rows, size), w_in[pl.ds(at, size), :], preferred_element_type=F32
        )
        if first:
            acc[c, h] = term
        else:
            acc[c, h] += term

    def add(ref, k, h, owner, first=False):
        at = pl.multiple_of(owner * xw + k % 2 * width, 128)
        accumulate(ref, k // 2, h, k % 2 * width, width, at, first)

    def own(k):
        for h in range(2):
            add(mine, k, h, x, first=k % 2 == 0)

    def sides(k):
        add(from_left, k, 0, left)
        add(from_right, k, 1, right)
        ring[k][2].wait_recv()
        add(from_left, k, 1, left)
        ring[k][3].wait_recv()
        add(from_right, k, 0, right)

    def opposite(k):
        ring[k][4].wait_recv()
        add(from_far, k, 0, far)
        ring[k][5].wait_recv()
        add(from_far, k, 1, far)

    def straight(c):
        y_own[4 + c].wait()
        wait_for(others(direct, c, 0, dw), y_recv.at[4 + c])
        for h in range(2):
            accumulate(direct, c, h, 0, dw, 4 * xw)

    def activate(c):
        for h in range(2):
            gate = acc[c, h, :, :ff]
            up = acc[c, h, :, ff:]
            hidden[c, h] = (gate / (1.0 + jnp.exp(-gate)) * up).astype(BF16)

    def down(c, s, h, owner):
        at = pl.multiple_of(owner * xw + s * stripe, 128)
        return jnp.dot(hidden[c, h], w_out[:, pl.ds(at, stripe)], preferred_element_type=F32)

    sums = {}

    def sum_start(c, s):
        sums[c, s] = [
            remote(
                partial.at[c, s, j],
                inbox.at[c, s, j],
                sum_send.at[c, s, j],
                sum_recv.at[c, s, j],
                {"half": right if j % 2 == 0 else left},
            )
            for j in range(6)
        ]
        for j, (owner, h) in enumerate([(far, 0), (far, 1), (right, 1), (left, 0)]):
            partial[c, s, j] = down(c, s, h, owner).astype(BF16)
            sums[c, s][j].start()

    def sum_middle(c, s):
        for j, (owner, h) in enumerate([(right, 0), (left, 1)]):
            term = down(c, s, h, owner)
            sums[c, s][j].wait_recv()
            partial[c, s, 4 + j] = (term + inbox[c, s, j].astype(F32)).astype(BF16)
            sums[c, s][4 + j].start()

    backs = {}

    def push_back(n, c, start, size):
        cols = pl.ds(start, size)
        there = returned.at[c, pl.ds(y * n_z, n_z), :, cols]

        @pl.loop(1, n_y)
        def _(i):
            peer = lax.rem(y + i, n_y)
            remote(
                done.at[c, pl.ds(peer * n_z, n_z), :, cols],
                there,
                back_send.at[n, c],
                back_recv.at[n, c],
                at_y(i),
            ).start()

        backs[n, c] = pltpu.make_async_copy(
            done.at[c, pl.ds(y * n_z, n_z), :, cols], there, back_local.at[n, c]
        )
        backs[n, c].start()

    def keep_done(c, h, start, size, term):
        done[c, h * half_groups : (h + 1) * half_groups, :, start : start + size] = term.astype(
            BF16
        ).reshape(half_groups, SLOTS, size)

    def sum_end(c, s):
        for h, near, through in ((0, 3, 4), (1, 2, 5)):
            term = down(c, s, h, x)
            sums[c, s][near].wait_recv()
            term = term + inbox[c, s, near].astype(F32)
            sums[c, s][through].wait_recv()
            term = term + inbox[c, s, through].astype(F32)
            keep_done(c, h, s * stripe, stripe, term)
        push_back(s, c, s * stripe, stripe)

    def straight_out(c):
        for h in range(2):
            term = jnp.dot(hidden[c, h], w_out[:, 4 * xw :], preferred_element_type=F32)
            keep_done(c, h, xw, dw, term)
        push_back(stripes, c, xw, dw)

    spans = [(s * stripe, stripe) for s in range(stripes)] + [(xw, dw)]
    downs = {}

    def combine(n):
        start, size = spans[n]
        cols = pl.ds(start, size)
        for c in range(2):
            backs[n, c].wait()
            wait_for(others(returned, c, start, size), back_recv.at[n, c])

        @pl.loop(0, n_z)
        def _(s):
            rows = jnp.concatenate(
                [
                    returned[c, q * n_z + s, :, start : start + size]
                    for c in range(2)
                    for q in range(n_y)
                ],
                axis=0,
            )
            both = jnp.dot(
                weights[s].reshape(2 * tokens, lanes), rows, preferred_element_type=F32
            )
            blend[s, :, start : start + size] = (both[:tokens] + both[tokens:]).astype(BF16)

        @pl.loop(1, n_z)
        def _(i):
            peer = lax.rem(z + i, n_z)
            remote(
                blend.at[peer, :, cols],
                landed.at[z, :, cols],
                down_send.at[n],
                down_recv.at[n],
                at_z(i),
            ).start()

        downs[n] = pltpu.make_async_copy(
            blend.at[z, :, cols], landed.at[z, :, cols], down_local.at[n]
        )
        downs[n].start()

    mixes = {}

    def exchange(n):
        start, size = spans[n]
        cols = pl.ds(start, size)
        downs[n].wait()
        wait_for(landed.at[pl.ds(0, n_z - 1), :, cols], down_recv.at[n])
        total = landed[0, :, start : start + size].astype(F32)
        for s in range(1, n_z):
            total = total + landed[s, :, start : start + size].astype(F32)
        piece[:, start : start + size] = total.astype(BF16)
        for j, where in enumerate((right, left, far)):
            mixes[n, j] = remote(
                piece.at[:, cols],
                gathered.at[j, :, cols],
                mix_send.at[n, j],
                mix_recv.at[n, j],
                {"half": where},
            )
            mixes[n, j].start()

    round_step(0, 0)
    own_select = push_control(0, select, chosen)
    round_step(1, 0)
    keep.wait()
    for step in range(1, plus):
        round_step(0, step)
        round_step(1, step)
    round_step(0, plus)
    round_step(2, 0)
    round_step(3, 0)
    wait_control(0, own_select, chosen)
    pick(0, width)
    push_y(0, 0, 0, width, mine, 0)
    round_step(1, plus)
    pick(width, width)
    push_y(1, 0, width, width, mine, width)
    push_y(2, 1, 0, width, mine, 0)
    push_y(3, 1, width, width, mine, width)
    round_step(2, 1)
    round_step(3, 1)
    arrive(0)
    round_step(2, 2)
    round_step(3, 2)
    for load in loads[:2]:
        load.wait()
    own(0)
    forward(0)
    arrive(1)
    for step in range(3, plus + 1):
        round_step(2, step)
        round_step(3, step)
    pick(xw, dw)
    push_y(4, 0, xw, dw, direct, 0)
    push_y(5, 1, xw, dw, direct, 0)
    own_gates = push_control(1, gates, weights)
    sides(0)
    arrive(2)
    own(1)
    forward(1)
    opposite(0)
    arrive(3)
    sides(1)
    own(2)
    opposite(1)
    straight(0)
    activate(0)
    loads[2].wait()
    sum_start(0, 0)
    forward(2)
    own(3)
    sum_start(0, 1)
    sum_middle(0, 0)
    forward(3)
    straight_out(0)
    sides(2)
    opposite(2)
    sum_start(0, 2)
    sum_middle(0, 1)
    sum_end(0, 0)
    straight(1)
    sides(3)
    opposite(3)
    activate(1)
    sum_start(1, 0)
    sum_middle(0, 2)
    straight_out(1)
    sum_start(1, 1)
    sum_end(0, 1)
    sum_middle(1, 0)
    sum_start(1, 2)
    sum_end(0, 2)
    sum_middle(1, 1)
    sum_end(1, 0)
    wait_control(1, own_gates, weights)
    combine(stripes)
    sum_middle(1, 2)
    combine(0)
    sum_end(1, 1)
    exchange(stripes)
    combine(1)
    sum_end(1, 2)
    exchange(0)
    exchange(1)
    combine(2)
    exchange(2)
    for n in range(stripes + 1):
        for j in range(3):
            mixes[n, j].wait_recv()
    result[:, pl.ds(pl.multiple_of(x * xw, 128), xw)] = piece[:, :xw]
    shared = piece[:, xw:].astype(F32)
    for j, owner in enumerate((left, right, far)):
        result[:, pl.ds(pl.multiple_of(owner * xw, 128), xw)] = gathered[j, :, :xw]
        shared = shared + gathered[j, :, xw:].astype(F32)
    result[:, 4 * xw :] = shared.astype(BF16)
    for p in range(4):
        for way, steps in ((0, plus), (1, minus)):
            for step in range(steps):
                trips[p, way, step].wait_send()
    wait_for(chosen.at[pl.ds(0, n_z - 1)], ctl_send.at[0])
    wait_for(weights.at[pl.ds(0, n_z - 1)], ctl_send.at[1])
    for k in range(4):
        wait_for(others(mine, k // 2, k % 2 * width, width), y_send.at[k])
        for j in range(6):
            ring[k][j].wait_send()
    for c in range(2):
        wait_for(others(direct, c, 0, dw), y_send.at[4 + c])
        for n, (start, size) in enumerate(spans):
            wait_for(others(returned, c, start, size), back_send.at[n, c])
        for s in range(stripes):
            for j in range(6):
                sums[c, s][j].wait_send()
    for n, (start, size) in enumerate(spans):
        wait_for(landed.at[pl.ds(0, n_z - 1), :, pl.ds(start, size)], down_send.at[n])
        for j in range(3):
            mixes[n, j].wait_send()


def experts(tok, select, gates, w_gate, w_up, w_down, n_ep, n_z, stripes):
    model, ff = w_gate.shape
    tokens, columns = tok.shape
    xw = (model - columns) // 3
    dw = columns - xw
    n_y = n_ep // n_z
    lanes = 2 * n_y * SLOTS
    half_rows = n_ep // 2 * SLOTS
    dma = pltpu.SemaphoreType.DMA
    vmem = pl.BlockSpec(memory_space=pltpu.VMEM)
    hbm = pl.BlockSpec(memory_space=pl.ANY)

    def space(*shape, dtype=BF16):
        return pltpu.VMEM(shape, dtype)

    return pl.pallas_call(
        moe_kernel,
        out_shape=jax.ShapeDtypeStruct((tokens, model), BF16),
        in_specs=[vmem, vmem, vmem, hbm, hbm, hbm],
        out_specs=vmem,
        scratch_shapes=[
            space(model, 2 * ff),
            space(ff, model),
            space(n_z, tokens, columns),
            space(n_z, 1, tokens, lanes),
            space(n_z, 2, tokens, lanes),
            space(2, n_y, n_z, SLOTS, columns),
            space(2, n_ep, SLOTS, xw),
            space(2, n_ep, SLOTS, dw),
            space(2, n_ep, SLOTS, xw),
            space(2, n_ep, SLOTS, xw),
            space(2, n_ep, SLOTS, xw),
            space(2, 2, half_rows, 2 * ff, dtype=F32),
            space(2, 2, half_rows, ff),
            space(2, stripes, 6, half_rows, xw // stripes),
            space(2, stripes, 6, half_rows, xw // stripes),
            space(2, n_ep, SLOTS, columns),
            space(2, n_ep, SLOTS, columns),
            space(n_z, tokens, columns),
            space(n_z, tokens, columns),
            space(tokens, columns),
            space(3, tokens, columns),
            dma((3,)),
            dma,
            dma((4, 2, n_z // 2)),
            dma((4, 2, n_z // 2)),
            dma((2,)),
            dma((2,)),
            dma((2,)),
            dma((6,)),
            dma((6,)),
            dma((6,)),
            dma((4, 6)),
            dma((4, 6)),
            dma((2, stripes, 6)),
            dma((2, stripes, 6)),
            dma((stripes + 1, 2)),
            dma((stripes + 1, 2)),
            dma((stripes + 1, 2)),
            dma((stripes + 1,)),
            dma((stripes + 1,)),
            dma((stripes + 1,)),
            dma((stripes + 1, 3)),
            dma((stripes + 1, 3)),
        ],
        compiler_params=pltpu.CompilerParams(
            collective_id=0, has_side_effects=True, vmem_limit_bytes=58 * 2**20
        ),
        cost_estimate=pl.CostEstimate(
            flops=12 * n_ep * SLOTS * model * ff,
            bytes_accessed=6 * model * ff + 500 * 2**20,
            transcendentals=2 * n_ep * SLOTS * ff,
        ),
        name="experts",
    )(tok, select, gates, w_gate, w_up, w_down)


def attend(block, prompt_lengths, query, fresh_key, fresh_value):
    group_tok = block.shape[0]
    group_rows = query.shape[0]
    position = jnp.arange(group_tok, dtype=jnp.int32)
    segment = (position >= prompt_lengths[0]).astype(jnp.int32)
    prompt = jnp.arange(group_rows, dtype=jnp.int32) // SAMPLES
    allowed = segment[None, :] == prompt[:, None]
    keys = block[:, :, 0, :]
    values = block[:, :, 1, :]
    scale = 1.0 / math.sqrt(HEAD)
    scores = jnp.einsum("rhgd,thd->rhgt", query, keys, preferred_element_type=F32) * scale
    scores = jnp.where(allowed[:, None, None, :], scores, -1e30)
    own = jnp.einsum("rhgd,rhd->rhg", query, fresh_key, preferred_element_type=F32) * scale
    top = jnp.maximum(jnp.max(scores, axis=3), own)
    spread = jnp.where(allowed[:, None, None, :], jnp.exp(scores - top[..., None]), 0.0)
    self_weight = jnp.exp(own - top)
    total = jnp.sum(spread, axis=3) + self_weight
    probs = (spread / total[..., None]).astype(BF16)
    self_prob = (self_weight / total).astype(BF16)
    mixed = jnp.einsum("rhgt,thd->rhgd", probs, values, preferred_element_type=F32)
    mixed = mixed + self_prob.astype(F32)[..., None] * fresh_value.astype(F32)[:, :, None, :]
    return mixed.astype(BF16).reshape(group_rows, -1)


def route(inputs, chosen, router, n_ep, n_z):
    count, top = chosen.shape
    pairs = count * top
    logits = jnp.dot(inputs, router, preferred_element_type=F32)
    onehot = chosen[:, :, None] == jnp.arange(n_ep, dtype=jnp.int32)
    picked = jnp.sum(jnp.where(onehot, logits[:, None, :], 0.0), axis=2)
    weights = jax.nn.softmax(picked, axis=1)
    flags = onehot.reshape(pairs, n_ep).astype(BF16)
    earlier = jnp.tri(pairs, pairs, -1, dtype=BF16)
    before = jnp.dot(earlier, flags, preferred_element_type=F32)
    rank = jnp.sum(before * flags.astype(F32), axis=1).astype(jnp.int32).reshape(count, top)
    n_y = n_ep // n_z
    place = (rank // SLOTS * n_y + chosen // n_z) * SLOTS + rank % SLOTS
    slot = chosen % n_z * (2 * n_y * SLOTS) + place
    select = slot[:, :, None] == jnp.arange(n_ep * CAP, dtype=jnp.int32)
    combine = jnp.sum(jnp.where(select, weights[:, :, None], 0.0), axis=1)
    coarse = combine.astype(BF16)
    fine = (combine - coarse.astype(F32)).astype(BF16)
    return jnp.any(select, axis=1).astype(BF16)[None], jnp.stack([coarse, fine])


def on_device(
    tokens,
    routes,
    router,
    w_gate,
    w_up,
    w_down,
    norm_gain,
    w_kv,
    lengths,
    queries,
    new_keys,
    new_values,
    w_out,
):
    inputs = tokens[0]
    n_ep = lax.axis_size("ep")
    own = inputs.shape[1] * 3 // 16
    select, gates = route(inputs, routes[0], router, n_ep, RING)
    part = lax.dynamic_slice_in_dim(inputs, lax.axis_index("half") * own, own, 1)
    tok = jnp.concatenate([part, inputs[:, 4 * own :]], axis=1)
    moe = experts(tok, select, gates, w_gate[0], w_up[0], w_down[0], n_ep, RING, 3)
    mixed = inputs.astype(F32) + moe.astype(F32)
    meansq = jnp.mean(mixed * mixed, axis=1, keepdims=True)
    normed = (mixed * lax.rsqrt(meansq + 1e-06) * norm_gain).astype(BF16)
    keyvals = jnp.dot(
        normed, lax.all_gather(w_kv, "ep", axis=0, tiled=True), preferred_element_type=F32
    ).astype(BF16)
    remote = lax.ppermute(keyvals, "pool", [(0, 1), (1, 0)])
    other = 1 - lax.axis_index("pool")
    prompt_lengths = lax.dynamic_index_in_dim(lengths, other, 0, keepdims=False)[0]
    kv_heads = new_keys.shape[2] // HEAD
    block = remote.reshape(remote.shape[0], kv_heads, 2, HEAD)
    query = queries[0].reshape(queries.shape[1], kv_heads, -1, HEAD)
    fresh_key = new_keys[0].reshape(new_keys.shape[1], kv_heads, HEAD)
    fresh_value = new_values[0].reshape(new_values.shape[1], kv_heads, HEAD)
    attention = attend(block, prompt_lengths, query, fresh_key, fresh_value)
    decoded = lax.psum_scatter(
        jnp.dot(attention, w_out, preferred_element_type=F32).astype(BF16),
        "half",
        scatter_dimension=0,
        tiled=True,
    )
    return decoded[None]


def solution(mesh):
    in_specs = (
        P("pool", "ep", None),
        P("pool", "ep", None),
        P(),
        P("ep", None, "half"),
        P("ep", None, "half"),
        P("ep", "half", None),
        P(),
        P("ep", "half"),
        P(None, "ep", None),
        P("pool", "ep", "half"),
        P("pool", "ep", "half"),
        P("pool", "ep", "half"),
        P("half", None),
    )
    out_specs = P("pool", ("ep", "half"), None)
    return jax.shard_map(
        on_device, mesh=mesh, in_specs=in_specs, out_specs=out_specs, check_vma=False
    )
```

time: 253 us -> 239 us (0.945)
  Pallas kernels: 190 us -> 178 us
  matrix products: 13.2 us -> 9.12 us
    pallas_call x1, Pallas kernels: 190 us -> 178 us  [experts(): pl.pallas_call(moe_kernel, out_shape=jax.ShapeDtypeStruct((tokens, model)...]
    dot_general x1 -> x0, matrix products: 3 us -> none  [on_device(): jnp.einsum('ts,td->sd', select, part, preferred_element_type=F32)]
  transfers between devices with their start and end apart: 3 -> 3, of which waited for: 2 -> 2; matrix products, arithmetic and copies ran while one was open for 8% -> 7% of each run, Pallas kernels for 75% -> 74%
where the time goes in v2:
time: 239 us
  Pallas kernels  178 us (74%)
  waiting for transfers between devices  25.4 us (11%)
  between operations  13.6 us (6%)
  matrix products  9.12 us (4%)
  other arithmetic  7.72 us (3%)
  local copies, waits for them, and re-layouts  5.12 us (2%)
    pallas_call x1, Pallas kernels, experts(): pl.pallas_call(moe_kernel, out_shape=jax.ShapeDtypeStruct((tokens, model)...  178 us
    reduce_scatter x1, waiting for transfers between devices, on_device(): lax.psum_scatter(jnp.dot(attention, w_out, preferred_element_type=F32).as...  24.5 us
  transfers between devices with their start and end apart: 3, of which 2 were waited for; matrix products, arithmetic and copies ran while one was open for 7% of the time, Pallas kernels for 74%

profile of v2, /device:TPU:8, one launch (start us, length us, event | category | flops | bytes accessed | tf_op | source)
XLA Modules:
  0.0 238.8 jit_solution(15698413778767958939)
XLA Ops:
  6.6 0.7 all-gather.2.cloned.1.call-update
  7.3 0.8 copy.28
  8.1 1.4 fusion.38
  9.5 0.7 select_reduce_fusion.1
  10.3 0.1 copy.31
  10.4 0.1 eq.55
  10.5 0.4 fusion.5
  10.9 0.1 convert_element_type.113
  11.0 0.9 slice.17
  11.9 1.0 reshape_squeeze.7
  13.0 0.8 reshape.236
  13.7 0.6 compare_convert_fusion
  14.4 0.6 and_select_fusion
  15.0 0.7 select_reduce_fusion
  15.8 0.7 pad_maximum_fusion.gates
  16.5 0.7 fusion
  17.2 0.7 convert_bitcast_fusion.select
  17.9 0.7 pad_maximum_fusion.1.tok
  18.6 177.7 %experts.1 = bf16[64,4096]{1,0:T(8,128)(2,1)} custom-call(bf16[64,1792]{1,0:T(8,128)(2,1)} %pad_maximum_fusion.1.tok, bf16[1,64,1024]{2,1,0:T(8,128)(2,1)} %convert_bitcast_fusion.select, bf16[2,64,1024]{2,1,0:T(8,128)(2,1)} %pad_maximum_fusion.gates, bf16[4096,384]{1,0:T(8,128)(2,1)} %bitcast.97, bf16[4096,384]{1,0:T(8,128)(2,1)} %bitcast.98, ...), custom_call_target="tpu_custom_call" | custom-call | flops 9663676416 | bytes 533725184 | tf_op jit(solution)/shard_map/experts/pallas_call | solution.py:558
  196.4 1.4 multiply_reduce_fusion
  197.8 0.5 add_rsqrt_fusion
  198.3 1.4 fusion.44
  199.7 3.7 %convolution_convert_fusion.1 = bf16[64,512]{1,0:T(8,128)(2,1)} fusion(bf16[4096,512]{1,0:T(8,128)(2,1)} %all-gather.2.cloned.1.call-done, bf16[64,4096]{1,0:T(8,128)(2,1)S(1)} %copy-done.2, f32[4096]{0:T(1024)S(1)} %copy-done.6, f32[64]{0:T(128)} %add_rsqrt_fusion, bf16[1,64,4096]{2,1,0:T(8,128)(2,1)S(1)} %copy-done.1), kind=kOutput, calls=%fused_computation.10 | convolution fusion | flops 270041088 | bytes 5325056 | tf_op jit(solution)/shard_map/dot_general | solution.py:690
  203.5 0.1 broadcast_compare_fusion
  203.6 1.1 copy.38
  204.6 0.1 copy.41
  204.7 0.2 collective-permute-done
  205.0 0.1 fusion.42
  205.1 0.2 fusion.43
  205.4 0.3 fusion.2
  205.7 1.7 convolution_convert_fusion
  207.4 24.5 %reduce-scatter.2.cloned.1.call-done = bf16[64,2048]{1,0:T(8,128)(2,1)} async-done(((bf16[256,2048]{1,0:T(8,128)(2,1)}), bf16[64,2048]{1,0:T(8,128)(2,1)}) %reduce-scatter.2.cloned.1.call-update) | async-done | bytes 262160 | tf_op jit(solution)/shard_map/reduce_scatter | solution.py:702
  (38 shorter events, 0.4 us)
Async XLA Ops:
  6.5 199.1 %copy-start = (bf16[512,2048]{1,0:T(8,128)(2,1)S(1)}, bf16[512,2048]{1,0:T(8,128)(2,1)}, u32[]{:S(2)}) copy-start(bf16[512,2048]{1,0:T(8,128)(2,1)} %param.25) | copy-start | bytes 6291460
  6.5 8.4 %copy-start.1 = (bf16[1,64,4096]{2,1,0:T(8,128)(2,1)S(1)}, bf16[1,64,4096]{2,1,0:T(8,128)(2,1)}, u32[]{:S(2)}) copy-start(bf16[1,64,4096]{2,1,0:T(8,128)(2,1)} %param.13) | copy-start | bytes 1572868
  6.5 6.4 %copy-start.4 = (bf16[1,256,256]{2,1,0:T(8,128)(2,1)S(1)}, bf16[1,256,256]{2,1,0:T(8,128)(2,1)}, u32[]{:S(2)}) copy-start(bf16[1,256,256]{2,1,0:T(8,128)(2,1)} %param.23) | copy-start | bytes 393220
  6.5 7.2 %copy-start.9 = (s32[2,1,2]{2,1,0:T(1,128)S(1)}, s32[2,1,2]{2,1,0:T(1,128)}, u32[]{:S(2)}) copy-start(s32[2,1,2]{2,1,0:T(1,128)} %param.21) | copy-start | bytes 52
  6.5 193.1 %all-gather.2.cloned.1.call-start = ((), (), s32[]{:S(2)}) async-start(), calls=%async_computation.1 | async-start | bytes 4325376 | tf_op jit(solution)/shard_map/all_gather | solution.py:691
  7.3 224.7 %reduce-scatter.2.cloned.1.call-start = ((), (), s32[]{:S(2)}) async-start(), calls=%async_computation.2 | async-start | bytes 1310720 | tf_op jit(solution)/shard_map/reduce_scatter | solution.py:702
  18.6 179.7 %copy-start.3 = (bf16[256,2,128,1]{2,3,1,0:T(2,128)(2,1)S(1)}, bf16[256,2,128,1]{2,3,1,0:T(2,128)(2,1)}, u32[]{:S(2)}) copy-start(bf16[256,2,128,1]{2,3,1,0:T(2,128)(2,1)} %reshape.236) | copy-start | bytes 393220
  196.4 3.3 %copy-start.2 = (bf16[64,4096]{1,0:T(8,128)(2,1)S(1)}, bf16[64,4096]{1,0:T(8,128)(2,1)}, u32[]{:S(2)}) copy-start(bf16[64,4096]{1,0:T(8,128)(2,1)} %experts.1) | copy-start | bytes 1572868
  196.4 3.3 %copy-start.6 = (f32[4096]{0:T(1024)S(1)}, f32[4096]{0:T(1024)}, u32[]{:S(2)}) copy-start(f32[4096]{0:T(1024)} %param.19) | copy-start | bytes 49156
  199.7 4.9 %copy-start.5 = (bf16[1,256,256]{2,1,0:T(8,128)(2,1)S(1)}, bf16[1,256,256]{2,1,0:T(8,128)(2,1)}, u32[]{:S(2)}) copy-start(bf16[1,256,256]{2,1,0:T(8,128)(2,1)} %param.24) | copy-start | bytes 393220
  199.7 3.8 %copy-start.7 = (s32[256]{0:T(256)S(1)}, s32[256]{0:T(256)}, u32[]{:S(2)}) copy-start(s32[256]{0:T(256)} %and_select_fusion) | copy-start | bytes 3076
  199.7 3.8 %copy-start.8 = (s32[64]{0:T(128)S(1)}, s32[64]{0:T(128)}, u32[]{:S(2)}) copy-start(s32[64]{0:T(128)} %compare_convert_fusion) | copy-start | bytes 772
  203.5 1.5 collective-permute-start
Sparse Core Ops, SparseCore 0:
  10.0 104.7 all-gather.1
  207.5 24.3 reduce-scatter.1

commit v3 on v2

--- a/solution.py
+++ b/solution.py
@@ -617,28 +617,150 @@
     )(tok, select, gates, w_gate, w_up, w_down)
 
 
-def attend(block, prompt_lengths, query, fresh_key, fresh_value):
-    group_tok = block.shape[0]
-    group_rows = query.shape[0]
-    position = jnp.arange(group_tok, dtype=jnp.int32)
-    segment = (position >= prompt_lengths[0]).astype(jnp.int32)
-    prompt = jnp.arange(group_rows, dtype=jnp.int32) // SAMPLES
-    allowed = segment[None, :] == prompt[:, None]
-    keys = block[:, :, 0, :]
-    values = block[:, :, 1, :]
+def decode_kernel(
+    tok,
+    moe,
+    gain,
+    w_kv,
+    allowed,
+    queries,
+    new_keys,
+    new_values,
+    w_out,
+    result,
+    w_kv_here,
+    w_out_here,
+    own_kv,
+    other_kv,
+    heads,
+    partial,
+    inbox,
+    load_sem,
+    swap_send,
+    swap_recv,
+    send_sem,
+    recv_sem,
+):
+    x = lax.axis_index("half")
+    right = lax.rem(x + 1, 4)
+    left = lax.rem(x + 3, 4)
+    far = lax.rem(x + 2, 4)
+    partner = {"pool": 1 - lax.axis_index("pool")}
+    load_kv = pltpu.make_async_copy(w_kv, w_kv_here, load_sem.at[0])
+    load_out = pltpu.make_async_copy(w_out, w_out_here, load_sem.at[1])
+    load_kv.start()
+    load_out.start()
+    barrier = pltpu.get_barrier_semaphore()
+    pl.semaphore_signal(barrier, inc=1, device_id=partner, device_id_type=MESH)
+    for peer in (left, right, far):
+        pl.semaphore_signal(barrier, inc=1, device_id={"half": peer}, device_id_type=MESH)
+
+    mixed = tok[...].astype(F32) + moe[...].astype(F32)
+    meansq = jnp.mean(mixed * mixed, axis=1, keepdims=True)
+    normed = (mixed * lax.rsqrt(meansq + 1e-06) * gain[...]).astype(BF16)
+    load_kv.wait()
+    own_kv[...] = jnp.dot(normed, w_kv_here[...], preferred_element_type=F32).astype(BF16)
+    pl.semaphore_wait(barrier, 4)
+    swap = pltpu.make_async_remote_copy(
+        src_ref=own_kv,
+        dst_ref=other_kv,
+        send_sem=swap_send,
+        recv_sem=swap_recv,
+        device_id=partner,
+        device_id_type=MESH,
+    )
+    swap.start()
+    rows = queries.shape[0] // 4
+    kv_heads = new_keys.shape[1] // HEAD
+    shared = queries.shape[1] // new_keys.shape[1]
     scale = 1.0 / math.sqrt(HEAD)
-    scores = jnp.einsum("rhgd,thd->rhgt", query, keys, preferred_element_type=F32) * scale
-    scores = jnp.where(allowed[:, None, None, :], scores, -1e30)
-    own = jnp.einsum("rhgd,rhd->rhg", query, fresh_key, preferred_element_type=F32) * scale
-    top = jnp.maximum(jnp.max(scores, axis=3), own)
-    spread = jnp.where(allowed[:, None, None, :], jnp.exp(scores - top[..., None]), 0.0)
-    self_weight = jnp.exp(own - top)
-    total = jnp.sum(spread, axis=3) + self_weight
-    probs = (spread / total[..., None]).astype(BF16)
-    self_prob = (self_weight / total).astype(BF16)
-    mixed = jnp.einsum("rhgt,thd->rhgd", probs, values, preferred_element_type=F32)
-    mixed = mixed + self_prob.astype(F32)[..., None] * fresh_value.astype(F32)[:, :, None, :]
-    return mixed.astype(BF16).reshape(group_rows, -1)
+    swap.wait_recv()
+    load_out.wait()
+
+    def block(owner):
+        at = pl.ds(pl.multiple_of(owner * rows, rows), rows)
+        seen = allowed[at, :] > 0.0
+        for h in range(kv_heads):
+            keys = other_kv[:, 2 * h * HEAD : (2 * h + 1) * HEAD]
+            values = other_kv[:, (2 * h + 1) * HEAD : (2 * h + 2) * HEAD]
+            fresh_key = new_keys[at, h * HEAD : (h + 1) * HEAD].astype(F32)
+            fresh_value = new_values[at, h * HEAD : (h + 1) * HEAD].astype(F32)
+            for g in range(shared):
+                cols = slice((h * shared + g) * HEAD, (h * shared + g + 1) * HEAD)
+                query = queries[at, cols]
+                scores = lax.dot_general(
+                    query, keys, (((1,), (1,)), ((), ())), preferred_element_type=F32
+                )
+                scores = jnp.where(seen, scores * scale, -1e30)
+                own = jnp.sum(query.astype(F32) * fresh_key, axis=1, keepdims=True) * scale
+                top = jnp.maximum(jnp.max(scores, axis=1, keepdims=True), own)
+                spread = jnp.where(seen, jnp.exp(scores - top), 0.0)
+                self_weight = jnp.exp(own - top)
+                total = jnp.sum(spread, axis=1, keepdims=True) + self_weight
+                probs = (spread / total).astype(BF16)
+                self_prob = (self_weight / total).astype(BF16).astype(F32)
+                value = jnp.dot(probs, values, preferred_element_type=F32)
+                heads[:, cols] = (value + self_prob * fresh_value).astype(BF16)
+        return jnp.dot(heads[...], w_out_here[...], preferred_element_type=F32)
+
+    copies = []
+    for j, owner in enumerate((far, right, left)):
+        partial[j] = block(owner).astype(BF16)
+        copy = pltpu.make_async_remote_copy(
+            src_ref=partial.at[j],
+            dst_ref=inbox.at[j],
+            send_sem=send_sem.at[j],
+            recv_sem=recv_sem.at[j],
+            device_id={"half": owner},
+            device_id_type=MESH,
+        )
+        copy.start()
+        copies.append(copy)
+    total = block(x).astype(BF16).astype(F32)
+    for j in (1, 2, 0):
+        copies[j].wait_recv()
+        total = total + inbox[j].astype(F32)
+    result[...] = total.astype(BF16)
+    swap.wait_send()
+    for copy in copies:
+        copy.wait_send()
+
+
+def decode(tok, moe, gain, w_kv, allowed, queries, new_keys, new_values, w_out):
+    rows, inner = queries.shape[0] // 4, queries.shape[1]
+    wide = w_out.shape[1]
+    dma = pltpu.SemaphoreType.DMA
+    vmem = pl.BlockSpec(memory_space=pltpu.VMEM)
+    hbm = pl.BlockSpec(memory_space=pl.ANY)
+    return pl.pallas_call(
+        decode_kernel,
+        out_shape=jax.ShapeDtypeStruct((rows, wide), BF16),
+        in_specs=[vmem, vmem, vmem, hbm, vmem, vmem, vmem, vmem, hbm],
+        out_specs=vmem,
+        scratch_shapes=[
+            pltpu.VMEM(w_kv.shape, BF16),
+            pltpu.VMEM(w_out.shape, BF16),
+            pltpu.VMEM((tok.shape[0], w_kv.shape[1]), BF16),
+            pltpu.VMEM((tok.shape[0], w_kv.shape[1]), BF16),
+            pltpu.VMEM((rows, inner), BF16),
+            pltpu.VMEM((3, rows, wide), BF16),
+            pltpu.VMEM((3, rows, wide), BF16),
+            dma((2,)),
+            dma,
+            dma,
+            dma((3,)),
+            dma((3,)),
+        ],
+        compiler_params=pltpu.CompilerParams(
+            collective_id=1, has_side_effects=True, vmem_limit_bytes=32 * 2**20
+        ),
+        cost_estimate=pl.CostEstimate(
+            flops=2 * tok.shape[0] * w_kv.size + 8 * rows * w_out.size,
+            bytes_accessed=2 * (w_kv.size + w_out.size),
+            transcendentals=8 * rows * tok.shape[0] * 8,
+        ),
+        name="decode",
+    )(tok, moe, gain, w_kv, allowed, queries, new_keys, new_values, w_out)
 
 
 def route(inputs, chosen, router, n_ep, n_z):
@@ -684,28 +806,17 @@
     part = lax.dynamic_slice_in_dim(inputs, lax.axis_index("half") * own, own, 1)
     tok = jnp.concatenate([part, inputs[:, 4 * own :]], axis=1)
     moe = experts(tok, select, gates, w_gate[0], w_up[0], w_down[0], n_ep, RING, 3)
-    mixed = inputs.astype(F32) + moe.astype(F32)
-    meansq = jnp.mean(mixed * mixed, axis=1, keepdims=True)
-    normed = (mixed * lax.rsqrt(meansq + 1e-06) * norm_gain).astype(BF16)
-    keyvals = jnp.dot(
-        normed, lax.all_gather(w_kv, "ep", axis=0, tiled=True), preferred_element_type=F32
-    ).astype(BF16)
-    remote = lax.ppermute(keyvals, "pool", [(0, 1), (1, 0)])
-    other = 1 - lax.axis_index("pool")
-    prompt_lengths = lax.dynamic_index_in_dim(lengths, other, 0, keepdims=False)[0]
-    kv_heads = new_keys.shape[2] // HEAD
-    block = remote.reshape(remote.shape[0], kv_heads, 2, HEAD)
-    query = queries[0].reshape(queries.shape[1], kv_heads, -1, HEAD)
-    fresh_key = new_keys[0].reshape(new_keys.shape[1], kv_heads, HEAD)
-    fresh_value = new_values[0].reshape(new_values.shape[1], kv_heads, HEAD)
-    attention = attend(block, prompt_lengths, query, fresh_key, fresh_value)
-    decoded = lax.psum_scatter(
-        jnp.dot(attention, w_out, preferred_element_type=F32).astype(BF16),
-        "half",
-        scatter_dimension=0,
-        tiled=True,
-    )
-    return decoded[None]
+    rows = w_kv.shape[0] // 2
+    pool = lax.axis_index("pool")
+    mine = lax.dynamic_slice_in_dim(w_kv, pool * rows, rows, 0)
+    w_all = lax.all_gather(mine, ("ep", "pool"), axis=0, tiled=True)
+    first = lax.dynamic_slice(lengths, (1 - pool, 0, 0), (1, 1, 1))[0]
+    second = jnp.arange(inputs.shape[0], dtype=jnp.int32)[None, :] >= first
+    prompt = jnp.arange(queries.shape[1], dtype=jnp.int32)[:, None] // SAMPLES
+    allowed = (second == (prompt == 1)).astype(F32)
+    return decode(
+        inputs, moe, norm_gain[None], w_all, allowed, queries[0], new_keys[0], new_values[0], w_out
+    )[None]
 
 
 def solution(mesh):

time: 239 us -> 224 us (0.937)
  waiting for transfers between devices: 25.4 us -> 0.04 us
  Pallas kernels: 178 us -> 193 us
  matrix products: 9.12 us -> 1.7 us
  local copies, waits for them, and re-layouts: 5.12 us -> 9.49 us
  other arithmetic: 7.72 us -> 5.15 us
    reduce_scatter x1 -> x0, waiting for transfers between devices: 24.5 us -> none  [on_device(): lax.psum_scatter(jnp.dot(attention, w_out, preferred_element_type=F32).as...]
    pallas_call x0 -> x1, Pallas kernels: none -> 18.5 us  [decode(): pl.pallas_call(decode_kernel, out_shape=jax.ShapeDtypeStruct((rows, wide)...]
    dot_general x5 -> x0, matrix products: 7.35 us -> none  [the longest x1 3.75 us: on_device(): jnp.dot(normed, lax.all_gather(w_kv, 'ep', axis=0, tiled=True), preferred...]
    unnamed x21 -> x20, local copies, waits for them, and re-layouts: 0.87 us -> 4.73 us
    pallas_call x1, Pallas kernels: 178 us -> 174 us  [experts(): pl.pallas_call(moe_kernel, out_shape=jax.ShapeDtypeStruct((tokens, model)...]
    dynamic_slice x1 -> x2, local copies, waits for them, and re-layouts: 0.01 us -> 2.67 us  [the longest x1 1.5 us: on_device(): mine = lax.dynamic_slice_in_dim(w_kv, pool * rows, rows, 0)]
  transfers between devices with their start and end apart: 3 -> 1, of which waited for: 2 -> 0; matrix products, arithmetic and copies ran while one was open for 7% -> 5% of each run, Pallas kernels for 74% -> 78%
where the time goes in v3:
time: 224 us; the launch traced here: 223 us
  Pallas kernels  193 us (86%)
  between operations  13.6 us (6%)
  local copies, waits for them, and re-layouts  9.49 us (4%)
  other arithmetic  5.15 us (2%)
    pallas_call x1, Pallas kernels, experts(): pl.pallas_call(moe_kernel, out_shape=jax.ShapeDtypeStruct((tokens, model)...  174 us
    pallas_call x1, Pallas kernels, decode(): pl.pallas_call(decode_kernel, out_shape=jax.ShapeDtypeStruct((rows, wide)...  18.5 us
    unnamed x20, local copies, waits for them, and re-layouts  4.73 us
  transfers between devices with their start and end apart: 1, of which 0 were waited for; matrix products, arithmetic and copies ran while one was open for 5% of the time, Pallas kernels for 78%

profile of v3, /device:TPU:8, one launch (start us, length us, event | category | flops | bytes accessed | tf_op | source)
XLA Modules:
  0.0 222.7 jit_solution(4947084165685369420)
XLA Ops:
  6.5 0.0 copy-start
  6.5 0.0 all-gather.2.cloned.1.call-start
  6.5 1.5 constant_dynamic-slice_fusion.1
  8.0 0.0 all-gather.2.cloned.1.call-update
  8.1 0.8 copy.20
  8.8 0.0 copy-done
  8.8 1.3 fusion.24
  10.1 0.7 select_reduce_fusion.1
  10.9 0.1 copy.23
  11.0 0.1 eq.60
  11.1 0.4 fusion.1
  11.5 0.1 convert_element_type.71
  11.6 0.9 slice.4
  12.6 1.2 constant_dynamic-slice_fusion
  13.7 0.6 iota_compare_fusion.6
  14.4 0.9 dynamic-slice_bitcast_fusion
  15.3 0.1 fusion.6
  15.4 0.7 select_reduce_fusion
  16.1 0.7 pad_maximum_fusion.gates
  16.9 0.7 fusion
  17.6 0.1 compare_convert_fusion.allowed
  17.7 0.7 convert_bitcast_fusion.select
  18.3 0.7 pad_maximum_fusion.1.tok
  19.0 0.0 copy-start.7
  19.1 0.0 copy-start.8
  19.1 174.3 %experts.1.moe = bf16[64,4096]{1,0:T(8,128)(2,1)} custom-call(bf16[64,1792]{1,0:T(8,128)(2,1)} %pad_maximum_fusion.1.tok, bf16[1,64,1024]{2,1,0:T(8,128)(2,1)} %convert_bitcast_fusion.select, bf16[2,64,1024]{2,1,0:T(8,128)(2,1)} %pad_maximum_fusion.gates, bf16[4096,384]{1,0:T(8,128)(2,1)} %bitcast.52, bf16[4096,384]{1,0:T(8,128)(2,1)} %bitcast.53, ...), custom_call_target="tpu_custom_call" | custom-call | flops 9663676416 | bytes 533725184 | tf_op jit(solution)/shard_map/experts/pallas_call | solution.py:558
  193.3 0.0 all-gather.2.cloned.1.call-done.w_kv
  193.4 0.0 copy-done.2
  193.4 2.2 copy-done.1
  195.6 1.0 copy-done.4
  196.7 18.5 %decode.1 = bf16[64,2048]{1,0:T(8,128)(2,1)S(1)} custom-call(bf16[64,4096]{1,0:T(8,128)(2,1)S(1)} %bitcast.45, bf16[64,4096]{1,0:T(8,128)(2,1)S(1)} %copy-done.4, f32[1,4096]{1,0:T(1,128)S(1)} %bitcast.50, bf16[4096,512]{1,0:T(8,128)(2,1)S(1)} %copy-done.1, f32[256,64]{1,0:T(8,128)S(1)} %compare_convert_fusion.allowed, bf16[256,512]{1,0:T(8,128)(2,1)S(1)} %bitcast.47, ...), custom_call_target="tpu_custom_call" | custom-call | flops 805306368 | bytes 6291456 | tf_op jit(solution)/shard_map/decode/pallas_call | solution.py:735
  215.2 0.7 copy.26
  (18 shorter events, 0.1 us)
Async XLA Ops:
  6.5 2.3 %copy-start = (bf16[4096,32]{0,1:T(8,128)(2,1)S(1)}, bf16[4096,32]{0,1:T(8,128)(2,1)}, u32[]{:S(2)}) copy-start(bf16[4096,32]{0,1:T(8,128)(2,1)} %param.15) | copy-start | bytes 786436
  6.5 186.8 %all-gather.2.cloned.1.call-start = ((), (), s32[]{:S(2)}) async-start(), calls=%async_computation | async-start | bytes 4259840 | tf_op jit(solution)/shard_map/all_gather | solution.py:812
  19.0 174.3 %copy-start.2 = (bf16[1,64,4096]{2,1,0:T(8,128)(2,1)S(1)}, bf16[1,64,4096]{2,1,0:T(8,128)(2,1)}, u32[]{:S(2)}) copy-start(bf16[1,64,4096]{2,1,0:T(8,128)(2,1)} %param.13) | copy-start | bytes 1572868
  19.0 174.3 %copy-start.3 = (bf16[512,2048]{1,0:T(8,128)(2,1)S(1)}, bf16[512,2048]{1,0:T(8,128)(2,1)}, u32[]{:S(2)}) copy-start(bf16[512,2048]{1,0:T(8,128)(2,1)} %w_out.1) | copy-start | bytes 6291460
  19.0 174.4 %copy-start.5 = (bf16[1,256,512]{2,1,0:T(8,128)(2,1)S(1)}, bf16[1,256,512]{2,1,0:T(8,128)(2,1)}, u32[]{:S(2)}) copy-start(bf16[1,256,512]{2,1,0:T(8,128)(2,1)} %param.22) | copy-start | bytes 786436
  19.0 174.4 %copy-start.6 = (bf16[1,256,256]{2,1,0:T(8,128)(2,1)S(1)}, bf16[1,256,256]{2,1,0:T(8,128)(2,1)}, u32[]{:S(2)}) copy-start(bf16[1,256,256]{2,1,0:T(8,128)(2,1)} %param.23) | copy-start | bytes 393220
  19.0 174.4 %copy-start.7 = (bf16[1,256,256]{2,1,0:T(8,128)(2,1)S(1)}, bf16[1,256,256]{2,1,0:T(8,128)(2,1)}, u32[]{:S(2)}) copy-start(bf16[1,256,256]{2,1,0:T(8,128)(2,1)} %param.24) | copy-start | bytes 393220
  19.1 174.4 %copy-start.8 = (f32[4096]{0:T(1024)S(1)}, f32[4096]{0:T(1024)}, u32[]{:S(2)}) copy-start(f32[4096]{0:T(1024)} %param.19) | copy-start | bytes 49156
  193.4 2.2 copy-start.1
  195.6 1.0 copy-start.4
Sparse Core Ops, SparseCore 0:
  10.1 86.2 all-gather.1

commit v4 on v3

--- a/solution.py
+++ b/solution.py
@@ -19,12 +19,15 @@
 
 def moe_kernel(
     tok,
-    select,
-    gates,
+    routes,
+    router,
     w_gate,
     w_up,
     w_down,
     result,
+    router_here,
+    select,
+    gates,
     w_in,
     w_out,
     held,
@@ -69,7 +72,8 @@
     mix_send,
     mix_recv,
 ):
-    tokens, columns = tok.shape
+    tokens = tok.shape[0]
+    columns = held.shape[2]
     xw = from_left.shape[3]
     dw = columns - xw
     width = xw // 2
@@ -103,8 +107,17 @@
     ]
     for load in loads:
         load.start()
-    keep = pltpu.make_async_copy(tok, held.at[z], tok_sem)
-    keep.start()
+    load_router = pltpu.make_async_copy(router, router_here, w_sem.at[3])
+    load_router.start()
+    own_cols = pl.ds(pl.multiple_of(x * xw, 128), xw)
+    keeps = [
+        pltpu.make_async_copy(tok.at[:, own_cols], held.at[z, :, pl.ds(0, xw)], tok_sem.at[0]),
+        pltpu.make_async_copy(
+            tok.at[:, pl.ds(4 * xw, dw)], held.at[z, :, pl.ds(xw, dw)], tok_sem.at[1]
+        ),
+    ]
+    for keep in keeps:
+        keep.start()
 
     barrier = pltpu.get_barrier_semaphore()
 
@@ -121,6 +134,56 @@
 
     for peer in (left, right, far):
         greet({"half": peer})
+
+    load_router.wait()
+    logits = lax.dot_general(
+        tok[...], router_here[...], (((1,), (1,)), ((), ())), preferred_element_type=F32
+    )
+    expert = lax.broadcasted_iota(jnp.int32, (n_ep, tokens), 0)
+    naming = jnp.zeros((n_ep, tokens), F32)
+    for k in range(routes.shape[0]):
+        naming = naming + jnp.where(routes[k : k + 1, :] == expert, 1.0, 0.0)
+    row = lax.broadcasted_iota(jnp.int32, (tokens, tokens), 0)
+    column = lax.broadcasted_iota(jnp.int32, (tokens, tokens), 1)
+
+    def by_token(pairs):
+        return lax.dot_general(
+            jnp.where(pairs, 1.0, 0.0).astype(BF16),
+            naming.astype(BF16),
+            (((1,), (1,)), ((), ())),
+            preferred_element_type=F32,
+        )
+
+    named = by_token(column == row)
+    rank = by_token(column < row)
+    top = jnp.max(jnp.where(named > 0.0, logits, -jnp.inf), axis=1, keepdims=True)
+    spread = jnp.where(named > 0.0, jnp.exp(jnp.minimum(logits - top, 0.0)), 0.0)
+    gate_of = spread / jnp.sum(spread, axis=1, keepdims=True)
+    coarse = gate_of.astype(BF16)
+    fine = (gate_of - coarse.astype(F32)).astype(BF16)
+
+    def bits(value, size):
+        return lax.shift_right_logical(value, jnp.int32(size.bit_length() - 1))
+
+    def slot_facts(count):
+        lane = lax.broadcasted_iota(jnp.int32, (count, n_ep * CAP), 1)
+        inner = lane & (lanes - 1)
+        whose = (bits(inner, SLOTS) & (n_y - 1)) * n_z + bits(lane, lanes)
+        return whose, bits(inner, n_y * SLOTS) * SLOTS + (inner & (SLOTS - 1))
+
+    whose, _ = slot_facts(n_ep)
+    spreader = jnp.where(
+        whose == lax.broadcasted_iota(jnp.int32, whose.shape, 0), 1.0, 0.0
+    ).astype(BF16)
+
+    def to_slots(table):
+        return jnp.dot(table.astype(BF16), spreader, preferred_element_type=F32)
+
+    _, place = slot_facts(tokens)
+    held_here = (to_slots(named) > 0.0) & (to_slots(rank) == place.astype(F32))
+    select[0] = jnp.where(held_here, 1.0, 0.0).astype(BF16)
+    gates[0] = jnp.where(held_here, to_slots(coarse), 0.0).astype(BF16)
+    gates[1] = jnp.where(held_here, to_slots(fine), 0.0).astype(BF16)
     pl.semaphore_wait(barrier, n_z + n_y + 1)
 
     def remote(src, dst, sems, recvs, where):
@@ -145,7 +208,11 @@
         cols = pl.ds(start, size)
         back = n_z - step if way == 0 else step
         block = lax.rem(z + back, n_z)
-        src = tok.at[:, cols] if step == 0 else held.at[block, :, cols]
+        if step == 0:
+            base = x * xw + start if start < xw else 3 * xw + start
+            src = tok.at[:, pl.ds(pl.multiple_of(base, 128), size)]
+        else:
+            src = held.at[block, :, cols]
         return remote(
             src,
             held.at[block, :, cols],
@@ -426,7 +493,8 @@
     round_step(0, 0)
     own_select = push_control(0, select, chosen)
     round_step(1, 0)
-    keep.wait()
+    for keep in keeps:
+        keep.wait()
     for step in range(1, plus):
         round_step(0, step)
         round_step(1, step)
@@ -479,7 +547,6 @@
     straight_out(0)
     sides(2)
     opposite(2)
-    sum_start(0, 2)
     sum_middle(0, 1)
     sum_end(0, 0)
     straight(1)
@@ -487,24 +554,25 @@
     opposite(3)
     activate(1)
     sum_start(1, 0)
-    sum_middle(0, 2)
+    sum_end(0, 1)
     straight_out(1)
+    sum_middle(1, 0)
     sum_start(1, 1)
-    sum_end(0, 1)
-    sum_middle(1, 0)
-    sum_start(1, 2)
-    sum_end(0, 2)
+    sum_start(0, 2)
+    sum_end(1, 0)
     sum_middle(1, 1)
-    sum_end(1, 0)
     wait_control(1, own_gates, weights)
     combine(stripes)
-    sum_middle(1, 2)
+    sum_start(1, 2)
+    sum_middle(0, 2)
     combine(0)
     sum_end(1, 1)
+    sum_end(0, 2)
+    sum_middle(1, 2)
     exchange(stripes)
     combine(1)
+    exchange(0)
     sum_end(1, 2)
-    exchange(0)
     exchange(1)
     combine(2)
     exchange(2)
@@ -540,11 +608,12 @@
             mixes[n, j].wait_send()
 
 
-def experts(tok, select, gates, w_gate, w_up, w_down, n_ep, n_z, stripes):
+def experts(tok, routes, router, w_gate, w_up, w_down, n_z, stripes):
     model, ff = w_gate.shape
-    tokens, columns = tok.shape
-    xw = (model - columns) // 3
-    dw = columns - xw
+    tokens, n_ep = tok.shape[0], router.shape[0]
+    xw = model * 3 // 16
+    dw = model - 4 * xw
+    columns = xw + dw
     n_y = n_ep // n_z
     lanes = 2 * n_y * SLOTS
     half_rows = n_ep // 2 * SLOTS
@@ -558,9 +627,12 @@
     return pl.pallas_call(
         moe_kernel,
         out_shape=jax.ShapeDtypeStruct((tokens, model), BF16),
-        in_specs=[vmem, vmem, vmem, hbm, hbm, hbm],
+        in_specs=[vmem, vmem, hbm, hbm, hbm, hbm],
         out_specs=vmem,
         scratch_shapes=[
+            space(n_ep, model),
+            space(1, tokens, n_ep * CAP),
+            space(2, tokens, n_ep * CAP),
             space(model, 2 * ff),
             space(ff, model),
             space(n_z, tokens, columns),
@@ -582,8 +654,8 @@
             space(n_z, tokens, columns),
             space(tokens, columns),
             space(3, tokens, columns),
-            dma((3,)),
-            dma,
+            dma((4,)),
+            dma((2,)),
             dma((4, 2, n_z // 2)),
             dma((4, 2, n_z // 2)),
             dma((2,)),
@@ -614,7 +686,7 @@
             transcendentals=2 * n_ep * SLOTS * ff,
         ),
         name="experts",
-    )(tok, select, gates, w_gate, w_up, w_down)
+    )(tok, routes, router, w_gate, w_up, w_down)
 
 
 def decode_kernel(
@@ -752,7 +824,7 @@
             dma((3,)),
         ],
         compiler_params=pltpu.CompilerParams(
-            collective_id=1, has_side_effects=True, vmem_limit_bytes=32 * 2**20
+            collective_id=1, has_side_effects=True, vmem_limit_bytes=58 * 2**20
         ),
         cost_estimate=pl.CostEstimate(
             flops=2 * tok.shape[0] * w_kv.size + 8 * rows * w_out.size,
@@ -761,27 +833,6 @@
         ),
         name="decode",
     )(tok, moe, gain, w_kv, allowed, queries, new_keys, new_values, w_out)
-
-
-def route(inputs, chosen, router, n_ep, n_z):
-    count, top = chosen.shape
-    pairs = count * top
-    logits = jnp.dot(inputs, router, preferred_element_type=F32)
-    onehot = chosen[:, :, None] == jnp.arange(n_ep, dtype=jnp.int32)
-    picked = jnp.sum(jnp.where(onehot, logits[:, None, :], 0.0), axis=2)
-    weights = jax.nn.softmax(picked, axis=1)
-    flags = onehot.reshape(pairs, n_ep).astype(BF16)
-    earlier = jnp.tri(pairs, pairs, -1, dtype=BF16)
-    before = jnp.dot(earlier, flags, preferred_element_type=F32)
-    rank = jnp.sum(before * flags.astype(F32), axis=1).astype(jnp.int32).reshape(count, top)
-    n_y = n_ep // n_z
-    place = (rank // SLOTS * n_y + chosen // n_z) * SLOTS + rank % SLOTS
-    slot = chosen % n_z * (2 * n_y * SLOTS) + place
-    select = slot[:, :, None] == jnp.arange(n_ep * CAP, dtype=jnp.int32)
-    combine = jnp.sum(jnp.where(select, weights[:, :, None], 0.0), axis=1)
-    coarse = combine.astype(BF16)
-    fine = (combine - coarse.astype(F32)).astype(BF16)
-    return jnp.any(select, axis=1).astype(BF16)[None], jnp.stack([coarse, fine])
 
 
 def on_device(
@@ -800,12 +851,7 @@
     w_out,
 ):
     inputs = tokens[0]
-    n_ep = lax.axis_size("ep")
-    own = inputs.shape[1] * 3 // 16
-    select, gates = route(inputs, routes[0], router, n_ep, RING)
-    part = lax.dynamic_slice_in_dim(inputs, lax.axis_index("half") * own, own, 1)
-    tok = jnp.concatenate([part, inputs[:, 4 * own :]], axis=1)
-    moe = experts(tok, select, gates, w_gate[0], w_up[0], w_down[0], n_ep, RING, 3)
+    moe = experts(inputs, routes[0].T, router.T, w_gate[0], w_up[0], w_down[0], RING, 3)
     rows = w_kv.shape[0] // 2
     pool = lax.axis_index("pool")
     mine = lax.dynamic_slice_in_dim(w_kv, pool * rows, rows, 0)

time: 224 us -> 209 us (0.933)
  Pallas kernels: 193 us -> 187 us
  local copies, waits for them, and re-layouts: 9.49 us -> 4.36 us
  other arithmetic: 5.15 us -> 1.41 us
    pallas_call x1, Pallas kernels: 174 us -> 165 us  [experts(): pl.pallas_call(moe_kernel, out_shape=jax.ShapeDtypeStruct((tokens, model)...]
    pallas_call x1, Pallas kernels: 18.5 us -> 22.2 us  [decode(): pl.pallas_call(decode_kernel, out_shape=jax.ShapeDtypeStruct((rows, wide)...]
    unnamed x20 -> x3, local copies, waits for them, and re-layouts: 4.73 us -> 2.57 us
  transfers between devices with their start and end apart: 1 -> 1, of which waited for: 0 -> 0; matrix products, arithmetic and copies ran while one was open for 5% -> 1% of each run, Pallas kernels for 78% -> 80%
where the time goes in v4:
time: 209 us; the launch traced here: 206 us
  Pallas kernels  187 us (89%)
  between operations  13.4 us (6%)
  local copies, waits for them, and re-layouts  4.36 us (2%)
    pallas_call x1, Pallas kernels, experts(): pl.pallas_call(moe_kernel, out_shape=jax.ShapeDtypeStruct((tokens, model)...  165 us
    pallas_call x1, Pallas kernels, decode(): pl.pallas_call(decode_kernel, out_shape=jax.ShapeDtypeStruct((rows, wide)...  22.2 us
  transfers between devices with their start and end apart: 1, of which 0 were waited for; matrix products, arithmetic and copies ran while one was open for 1% of the time, Pallas kernels for 80%

profile of v4, /device:TPU:8, one launch (start us, length us, event | category | flops | bytes accessed | tf_op | source)
XLA Modules:
  0.0 206.5 jit_solution(4460545297511319294)
XLA Ops:
  6.5 0.0 copy-start
  6.5 0.0 all-gather.2.cloned.1.call-start
  6.5 0.9 copy-done
  7.4 0.6 constant_dynamic-slice_fusion.1
  8.1 0.0 all-gather.2.cloned.1.call-update
  8.1 1.2 constant_dynamic-slice_fusion
  9.3 0.6 iota_compare_fusion
  9.9 0.8 compare_convert_fusion.allowed
  10.7 165.1 %experts.1.moe = bf16[64,4096]{1,0:T(8,128)(2,1)} custom-call(bf16[64,4096]{1,0:T(8,128)(2,1)} %bitcast.15, s32[8,64]{1,0:T(8,128)} %bitcast.25, bf16[32,4096]{1,0:T(8,128)(2,1)} %bitcast.24, bf16[4096,384]{1,0:T(8,128)(2,1)} %bitcast.21, bf16[4096,384]{1,0:T(8,128)(2,1)} %bitcast.22, bf16[384,4096]{1,0:T(8,128)(2,1)} %bitcast.23), custom_call_target="tpu_custom_call" | custom-call | flops 9663676416 | bytes 533725184 | tf_op jit(solution)/shard_map/experts/pallas_call | solution.py:627
  175.8 0.0 all-gather.2.cloned.1.call-done.w_kv
  175.8 22.2 %decode.1 = bf16[64,2048]{1,0:T(8,128)(2,1)} custom-call(bf16[64,4096]{1,0:T(8,128)(2,1)} %bitcast.16, bf16[64,4096]{1,0:T(8,128)(2,1)} %experts.1.moe, f32[1,4096]{1,0:T(1,128)} %bitcast.20, bf16[4096,512]{1,0:T(8,128)(2,1)} %all-gather.2.cloned.1.call-done.w_kv, f32[256,64]{1,0:T(8,128)} %compare_convert_fusion.allowed, bf16[256,512]{1,0:T(8,128)(2,1)} %bitcast.17, ...), custom_call_target="tpu_custom_call" | custom-call | flops 805306368 | bytes 6291456 | tf_op jit(solution)/shard_map/decode/pallas_call | solution.py:807
  198.0 1.7 copy.15
  (1 shorter events, 0.0 us)
Async XLA Ops:
  6.5 0.9 copy-start
  6.5 169.2 %all-gather.2.cloned.1.call-start = ((), (), s32[]{:S(2)}) async-start(), calls=%async_computation | async-start | bytes 4259840 | tf_op jit(solution)/shard_map/all_gather | solution.py:858
Sparse Core Ops, SparseCore 0:
  10.1 83.9 all-gather.1

commit v5 on v4

--- a/solution.py
+++ b/solution.py
@@ -505,23 +505,25 @@
     pick(0, width)
     push_y(0, 0, 0, width, mine, 0)
     round_step(1, plus)
+    round_step(2, 1)
+    round_step(3, 1)
     pick(width, width)
     push_y(1, 0, width, width, mine, width)
     push_y(2, 1, 0, width, mine, 0)
     push_y(3, 1, width, width, mine, width)
-    round_step(2, 1)
-    round_step(3, 1)
-    arrive(0)
     round_step(2, 2)
     round_step(3, 2)
+    arrive(0)
+    for step in range(3, plus):
+        round_step(2, step)
+        round_step(3, step)
     for load in loads[:2]:
         load.wait()
     own(0)
+    round_step(2, plus)
+    round_step(3, plus)
     forward(0)
     arrive(1)
-    for step in range(3, plus + 1):
-        round_step(2, step)
-        round_step(3, step)
     pick(xw, dw)
     push_y(4, 0, xw, dw, direct, 0)
     push_y(5, 1, xw, dw, direct, 0)

time: 209 us -> 216 us (1.033)
  Pallas kernels: 187 us -> 193 us
    pallas_call x1, Pallas kernels: 165 us -> 173 us  [experts(): pl.pallas_call(moe_kernel, out_shape=jax.ShapeDtypeStruct((tokens, model)...]
  transfers between devices with their start and end apart: 1 -> 1, of which waited for: 0 -> 0; matrix products, arithmetic and copies ran while one was open for 1% -> 1% of each run, Pallas kernels for 80% -> 81%
where the time goes in v5:
time: 216 us; the launch traced here: 213 us
  Pallas kernels  193 us (89%)
  between operations  13.4 us (6%)
  local copies, waits for them, and re-layouts  4.36 us (2%)
    pallas_call x1, Pallas kernels, experts(): pl.pallas_call(moe_kernel, out_shape=jax.ShapeDtypeStruct((tokens, model)...  173 us
    pallas_call x1, Pallas kernels, decode(): pl.pallas_call(decode_kernel, out_shape=jax.ShapeDtypeStruct((rows, wide)...  20.2 us
  transfers between devices with their start and end apart: 1, of which 0 were waited for; matrix products, arithmetic and copies ran while one was open for 1% of the time, Pallas kernels for 81%

profile of v5, /device:TPU:8, one launch (start us, length us, event | category | flops | bytes accessed | tf_op | source)
XLA Modules:
  0.0 212.6 jit_solution(14115208394101267312)
XLA Ops:
  6.5 0.0 copy-start
  6.5 0.0 all-gather.2.cloned.1.call-start
  6.5 0.9 copy-done
  7.4 0.6 constant_dynamic-slice_fusion.1
  8.1 0.0 all-gather.2.cloned.1.call-update
  8.1 1.2 constant_dynamic-slice_fusion
  9.3 0.6 iota_compare_fusion
  9.9 0.8 compare_convert_fusion.allowed
  10.7 173.1 %experts.1.moe = bf16[64,4096]{1,0:T(8,128)(2,1)} custom-call(bf16[64,4096]{1,0:T(8,128)(2,1)} %bitcast.15, s32[8,64]{1,0:T(8,128)} %bitcast.25, bf16[32,4096]{1,0:T(8,128)(2,1)} %bitcast.24, bf16[4096,384]{1,0:T(8,128)(2,1)} %bitcast.21, bf16[4096,384]{1,0:T(8,128)(2,1)} %bitcast.22, bf16[384,4096]{1,0:T(8,128)(2,1)} %bitcast.23), custom_call_target="tpu_custom_call" | custom-call | flops 9663676416 | bytes 533725184 | tf_op jit(solution)/shard_map/experts/pallas_call | solution.py:629
  183.8 0.0 all-gather.2.cloned.1.call-done.w_kv
  183.8 20.2 %decode.1 = bf16[64,2048]{1,0:T(8,128)(2,1)} custom-call(bf16[64,4096]{1,0:T(8,128)(2,1)} %bitcast.16, bf16[64,4096]{1,0:T(8,128)(2,1)} %experts.1.moe, f32[1,4096]{1,0:T(1,128)} %bitcast.20, bf16[4096,512]{1,0:T(8,128)(2,1)} %all-gather.2.cloned.1.call-done.w_kv, f32[256,64]{1,0:T(8,128)} %compare_convert_fusion.allowed, bf16[256,512]{1,0:T(8,128)(2,1)} %bitcast.17, ...), custom_call_target="tpu_custom_call" | custom-call | flops 805306368 | bytes 6291456 | tf_op jit(solution)/shard_map/decode/pallas_call | solution.py:809
  204.0 1.7 copy.15
  (1 shorter events, 0.0 us)
Async XLA Ops:
  6.5 0.9 copy-start
  6.5 177.3 %all-gather.2.cloned.1.call-start = ((), (), s32[]{:S(2)}) async-start(), calls=%async_computation | async-start | bytes 4259840 | tf_op jit(solution)/shard_map/all_gather | solution.py:860
Sparse Core Ops, SparseCore 0:
  10.1 86.1 all-gather.1
